TPU v7x, 512 devices: a whole 4x4x16 slice. The times are simulated.
512 devices in a mesh: group: 8 (over x, core), rank: 64 (over z, y).
Axes of the slice: x: 4, y: 4, z: 16, core: 2. Of those that a mesh axis runs over, the one named last changes fastest.
Arguments:
- degree: int32 [65536], P(('group', 'rank')), may hold values from 2 to 5
- curve_order: int32 [512, 128], P(('group', 'rank')), may hold values from 0 to 127, each once within a row
- neighbours: int32 [6, 65536], P(None, ('group', 'rank')), may hold values from 0 to 65535, as said below
- coupling: float32 [6, 65536], P(None, ('group', 'rank')), may hold values from 0.03 to 0.2
- stiffness: float32 [65536], P(('group', 'rank')), may hold values from 0.1 to 1
- lame: float32 [65536], P(('group', 'rank')), may hold values from 0.05 to 0.5
- load: float32 [3, 6, 6, 6, 65536], P(None, None, None, None, ('group', 'rank')), may hold values from -6 to 6
Outputs:
- owner: int32 [65536], P(('group', 'rank'))
- smoothed: float32 [3, 6, 6, 6, 65536], P(None, None, None, None, ('group', 'rank'))
Inputs may be any that keep to these rules, and one draw needn't show every extreme that they name: `curve_order`: every row is a permutation of 0 to 127. `neighbours`: each listed neighbour lies 1 to 32 positions away along the curve from its cell; every cell's first listed neighbour lies exactly 32 positions away.
All inputs are finite; a program needn't handle non-finite values.
Results may differ from a plain program's by a relative error of at most 0.0003.
Values sent between devices are 32-bit elements; how exact they have to be, the bound alone decides.
No kernel may reach another device: no remote copies, remote signals or barrier semaphores. Data moves between devices by JAX's collectives and lax.ppermute only.
A program may use at most 128 MiB of HBM per device.

v0:
```python
import jax
import jax.numpy as jnp
from jax import lax
from jax.sharding import PartitionSpec as P

NODES = 6
COMPONENTS = 3
REACH = 32
SWEEPS = 2
DEGREE = 3


def entering(part, axis, combine, identity):
    place = lax.axis_index(axis)
    gathered = lax.all_gather(part, axis)
    state = jnp.zeros_like(part) + jnp.asarray(identity, part.dtype)

    def one(turn, state):
        return combine(state, lax.dynamic_index_in_dim(gathered, turn, 0, False))

    return lax.fori_loop(0, place, one, state)


def extended_2(array, sides, width):
    for axis, dim in sides:
        size, length = (lax.axis_size(axis), array.shape[dim])
        up = [(i, (i + 1) % size) for i in range(size - 1)]
        down = [(j, i) for i, j in up]
        last = lax.slice_in_dim(array, length - width, length, axis=dim)
        initial = lax.slice_in_dim(array, 0, width, axis=dim)
        before = lax.ppermute(last, axis, up)
        after = lax.ppermute(initial, axis, down)
        array = jnp.concatenate([before, array, after], axis=dim)
    return array


def mass_table():
    spots = jnp.arange(NODES)
    beside = jnp.abs(spots[:, None] - spots[None, :]) == 1
    return jnp.where(beside, 0.15, 0.0).astype(jnp.float32) + jnp.eye(NODES, dtype=jnp.float32)


def stiff_table():
    spots = jnp.arange(NODES)
    beside = jnp.abs(spots[:, None] - spots[None, :]) == 1
    return jnp.where(beside, -1.0, 0.0).astype(jnp.float32) + 2.0 * jnp.eye(
        NODES, dtype=jnp.float32
    )


def along(table, field, which):
    forms = {1: "ip,apjkc->aijkc", 2: "jp,aipkc->aijkc", 3: "kp,aijpc->aijkc"}
    return jnp.einsum(forms[which], table, field, precision=lax.Precision.HIGHEST)


def local_part(field, stiffness, lame):
    mass = mass_table()
    stiff = stiff_table()
    mixing = (
        jnp.ones((COMPONENTS, COMPONENTS), jnp.float32) + jnp.eye(COMPONENTS, dtype=jnp.float32)
    ) * 0.5
    after_z = along(mass, field, 3)
    after_yz = along(mass, after_z, 2)
    term_x = along(stiff, after_yz, 1)
    full_mass = along(mass, after_yz, 1)
    term_y = along(stiff, along(mass, after_z, 1), 2)
    term_z = along(stiff, along(mass, along(mass, field, 2), 1), 3)
    mixed = jnp.einsum("ab,bijkc->aijkc", mixing, full_mass, precision=lax.Precision.HIGHEST)
    return stiffness * (term_x + term_y + term_z) + lame * mixed


def node_mask(cdeg):
    spots = jnp.arange(NODES, dtype=jnp.int32)
    first = spots[:, None] <= cdeg[None, :]
    inside = first[:, None, None, :] & first[None, :, None, :] & first[None, None, :, :]
    return inside[None].astype(jnp.float32)


def add_counts(earlier, later):
    return earlier + later


def weighted_table(slots, values, width):
    columns = jnp.arange(width, dtype=jnp.int32)
    hits = (slots[:, :, None] == columns[None, None, :]).astype(jnp.float32)
    return jnp.sum(values[:, :, None] * hits, axis=0)


def shards(degree, curve_order, neighbours, coupling, stiffness, lame, load):
    cells = degree.shape[0]
    order = curve_order[0]
    cdeg = jnp.take(degree, order)
    rhs = jnp.take(load, order, axis=4)
    weight = (cdeg + 1) ** 3
    inclusive = jnp.cumsum(weight).astype(jnp.int32)
    local_total = inclusive[-1]
    devices = lax.axis_size("group") * lax.axis_size("rank")
    position = lax.axis_index("group") * lax.axis_size("rank") + lax.axis_index("rank")
    total = lax.psum(local_total, ("group", "rank"))
    before = entering(local_total, ("group", "rank"), add_counts, jnp.int32(0)).astype(jnp.int32)
    share = (total + devices - 1) // devices
    owner = ((before + inclusive - weight) // share).astype(jnp.int32)
    mask = node_mask(cdeg)
    inverse = mask / (6.0 * stiffness + lame)
    count = coupling.shape[0]
    extended = cells + 2 * REACH
    base = position * cells
    statics = jnp.concatenate([coupling, stiffness[None, :]], 0)
    rims = extended_2(statics, ((("group", "rank"), 1),), REACH)
    stiff_ext = rims[count]
    spot = neighbours - base + REACH
    other = jnp.take(stiff_ext, spot)
    pull_weights = coupling * (2.0 * stiffness[None, :] * other / (stiffness[None, :] + other))
    pull_table = weighted_table(spot, pull_weights, extended)

    def operate(field):
        flat = field.reshape(-1, cells)
        field_ext = extended_2(flat, ((("group", "rank"), 1),), REACH)
        local = local_part(field, stiffness, lame)
        pulled = jnp.dot(field_ext, pull_table.T, precision=lax.Precision.HIGHEST)
        bucket = jnp.dot(flat, pull_table, precision=lax.Precision.HIGHEST)
        edges = jnp.concatenate([bucket[:, :REACH], bucket[:, REACH + cells :]], 1)
        returned = extended_2(edges, ((("group", "rank"), 1),), REACH)
        pushed = bucket[:, REACH : REACH + cells]
        pushed = pushed.at[:, :REACH].add(returned[:, :REACH])
        pushed = pushed.at[:, cells - REACH :].add(returned[:, 3 * REACH :])
        couple = (pulled + pushed).reshape(field.shape)
        return mask * (local - couple)

    theta = (5.0 + 0.5) / 2.0
    delta = (5.0 - 0.5) / 2.0
    sigma = theta / delta
    smoothed = jnp.zeros_like(rhs)
    for sweep in range(SWEEPS):
        rho_old = 1.0 / sigma
        if sweep == 0:
            resid = rhs
        else:
            resid = rhs - operate(smoothed)
        step = inverse * resid / theta
        smoothed = smoothed + step
        for inner in range(DEGREE - 1):
            rho = 1.0 / (2.0 * sigma - rho_old)
            resid = rhs - operate(smoothed)
            step = rho * rho_old * step + 2.0 * rho / delta * inverse * resid
            smoothed = smoothed + step
            rho_old = rho
    return (owner, smoothed)


def solution(mesh):
    return jax.shard_map(
        shards,
        mesh=mesh,
        in_specs=(
            P(("group", "rank")),
            P(("group", "rank"), None),
            P(None, ("group", "rank")),
            P(None, ("group", "rank")),
            P(("group", "rank")),
            P(("group", "rank")),
            P(None, None, None, None, ("group", "rank")),
        ),
        out_specs=(P(("group", "rank")), P(None, None, None, None, ("group", "rank"))),
        check_vma=False,
    )
```

profile of v0, /device:TPU:487, one launch (start us, length us, event | category | flops | bytes accessed | tf_op | source)
XLA Modules:
  0.0 999.2 jit_solution(16764501085516538662)
XLA Ops:
  1.4 5.1 collective-permute-start.3
  13.3 6.8 copy.127
  20.1 9.1 gather_fusion.1
  29.2 5.5 reshape.476
  35.9 5.5 collective-permute-start.1
  43.4 5.7 copy.128
  53.0 104.0 %all-reduce.1 = (s32[512]{0:T(512)S(1)}, s32[]{:T(128)}) all-reduce(s32[512]{0:T(512)S(1)} %bitcast_dynamic-update-slice_fusion, s32[]{:T(128)} %bitcast.6), channel_id=2, replica_groups=mesh['group'=8,'rank'=64] {'group','rank'}, use_global_device_ids=true, to_apply=%add | all-reduce | flops 513 | bytes 4104 | tf_op jit(solution)/shard_map/all_gather | solution.py:15
  157.0 648.0 %while.20 = (s32[]{:T(128)}, s32[]{:T(128)}, s32[]{:T(128)}, s32[512]{0:T(512)S(1)}, s32[]{:T(128)}, /*index=5*/s32[]{:T(128)}, s32[]{:T(128)}) while((s32[]{:T(128)}, s32[]{:T(128)}, s32[]{:T(128)}, s32[512]{0:T(512)S(1)}, s32[]{:T(128)}, /*index=5*/s32[]{:T(128)}, s32[]{:T(128)}) %tuple.83), condition=%wide.region_2.3_spmd, body=%wide.region_1.2_spmd.sunk | while | flops 6 | bytes 143 | solution.py:21
  810.1 5.0 gather_fusion.2
  821.1 4.7 collective-permute-start.5
  832.3 3.5 scatter-add.35
  844.8 6.0 collective-permute-start.8
  854.8 3.7 collective-permute-start.6
  870.1 3.8 scatter-add.39
  884.7 3.3 collective-permute-start.12
  888.1 4.0 collective-permute-start.13
  894.2 3.4 collective-permute-start.10
  908.4 3.8 scatter-add.41
  925.5 5.4 collective-permute-start.17
  933.1 3.4 collective-permute-start.14
  948.1 3.8 scatter-add.45
  965.4 5.5 collective-permute-start.21
  973.0 3.5 collective-permute-start.18
  987.3 3.8 scatter-add.49
  (696 shorter events, 455.1 us)
Async XLA Ops:
  1.4 808.5 %collective-permute-start.3 = (f32[7,32]{1,0:T(8,128)S(1)}, f32[7,32]{1,0:T(8,128)S(1)}, u32[]{:S(2)}, u32[]{:S(2)}) collective-permute-start(f32[7,32]{1,0:T(8,128)S(1)} %get-tuple-element.188), channel_id=1, source_target_pairs={{1,0},{2,1},{3,2},{4,3},{5,4},{6,5},{7,6},{8,7},{9,8},{10,9},{11,1... | collective-permute-start | bytes 2696 | tf_op jit(solution)/shard_map/ppermute | solution.py:32
  6.5 803.5 %collective-permute-start.2 = (f32[7,32]{1,0:T(8,128)S(1)}, f32[7,32]{1,0:T(8,128)S(1)}, u32[]{:S(2)}, u32[]{:S(2)}) collective-permute-start(f32[7,32]{1,0:T(8,128)S(1)} %get-tuple-element.187), channel_id=1, source_target_pairs={{0,1},{1,2},{2,3},{3,4},{4,5},{5,6},{6,7},{7,8},{8,9},{9,10},{10,1... | collective-permute-start | bytes 2696 | tf_op jit(solution)/shard_map/ppermute | solution.py:31
  34.8 770.4 %copy-start.8 = (s32[6,128]{1,0:T(8,128)S(1)}, s32[6,128]{1,0:T(8,128)}, u32[]{:S(2)}) copy-start(s32[6,128]{1,0:T(8,128)} %param.31) | copy-start | bytes 9220
  35.9 799.8 %collective-permute-start.1 = (f32[648,32]{1,0:T(8,128)}, f32[648,32]{1,0:T(8,128)}, u32[]{:S(2)}, u32[]{:S(2)}) collective-permute-start(f32[648,32]{1,0:T(8,128)} %get-tuple-element.181), channel_id=1, source_target_pairs={{1,0},{2,1},{3,2},{4,3},{5,4},{6,5},{7,6},{8,7},{9,8},{10,9},{11,1... | collective-permute-start | bytes 248840 | tf_op jit(solution)/shard_map/ppermute | solution.py:32
  41.4 794.4 %collective-permute-start = (f32[648,32]{1,0:T(8,128)}, f32[648,32]{1,0:T(8,128)}, u32[]{:S(2)}, u32[]{:S(2)}) collective-permute-start(f32[648,32]{1,0:T(8,128)} %get-tuple-element.180), channel_id=1, source_target_pairs={{0,1},{1,2},{2,3},{3,4},{4,5},{5,6},{6,7},{7,8},{8,9},{9,10},{10,1... | collective-permute-start | bytes 248840 | tf_op jit(solution)/shard_map/ppermute | solution.py:31
  51.5 786.2 %copy-start.7 = (f32[128]{0:T(128)S(1)}, f32[128]{0:T(128)}, u32[]{:S(2)}) copy-start(f32[128]{0:T(128)} %param.34) | copy-start | bytes 1540
  816.7 10.9 %collective-permute-start.4 = (f32[648,32]{1,0:T(8,128)S(1)}, f32[648,32]{1,0:T(8,128)S(1)}, u32[]{:S(2)}, u32[]{:S(2)}) collective-permute-start(f32[648,32]{1,0:T(8,128)S(1)} %get-tuple-element.171), channel_id=1, source_target_pairs={{0,1},{1,2},{2,3},{3,4},{4,5},{5,6},{6,7},{7,8},{8,9},{9,10},{10,1... | collective-permute-start | bytes 248840 | tf_op jit(solution)/shard_map/ppermute | solution.py:31
  821.1 10.0 %collective-permute-start.5 = (f32[648,32]{1,0:T(8,128)}, f32[648,32]{1,0:T(8,128)}, u32[]{:S(2)}, u32[]{:S(2)}) collective-permute-start(f32[648,32]{1,0:T(8,128)} %get-tuple-element.170), channel_id=1, source_target_pairs={{1,0},{2,1},{3,2},{4,3},{5,4},{6,5},{7,6},{8,7},{9,8},{10,9},{11,1... | collective-permute-start | bytes 248840 | tf_op jit(solution)/shard_map/ppermute | solution.py:32
  844.8 18.7 %collective-permute-start.8 = (f32[648,32]{1,0:T(8,128)S(1)}, f32[648,32]{1,0:T(8,128)S(1)}, u32[]{:S(2)}, u32[]{:S(2)}) collective-permute-start(f32[648,32]{1,0:T(8,128)S(1)} %get-tuple-element.169), channel_id=1, source_target_pairs={{0,1},{1,2},{2,3},{3,4},{4,5},{5,6},{6,7},{7,8},{8,9},{9,10},{10,1... | collective-permute-start | bytes 248840 | tf_op jit(solution)/shard_map/ppermute | solution.py:31
  850.8 17.4 %collective-permute-start.9 = (f32[648,32]{1,0:T(8,128)}, f32[648,32]{1,0:T(8,128)}, u32[]{:S(2)}, u32[]{:S(2)}) collective-permute-start(f32[648,32]{1,0:T(8,128)} %get-tuple-element.168), channel_id=1, source_target_pairs={{1,0},{2,1},{3,2},{4,3},{5,4},{6,5},{7,6},{8,7},{9,8},{10,9},{11,1... | collective-permute-start | bytes 248840 | tf_op jit(solution)/shard_map/ppermute | solution.py:32
  852.7 21.1 %collective-permute-start.7 = (f32[648,32]{1,0:T(8,128)}, f32[648,32]{1,0:T(8,128)}, u32[]{:S(2)}, u32[]{:S(2)}) collective-permute-start(f32[648,32]{1,0:T(8,128)} %get-tuple-element.179), channel_id=1, source_target_pairs={{1,0},{2,1},{3,2},{4,3},{5,4},{6,5},{7,6},{8,7},{9,8},{10,9},{11,1... | collective-permute-start | bytes 248840 | tf_op jit(solution)/shard_map/ppermute | solution.py:32
  854.8 19.1 %collective-permute-start.6 = (f32[648,32]{1,0:T(8,128)}, f32[648,32]{1,0:T(8,128)}, u32[]{:S(2)}, u32[]{:S(2)}) collective-permute-start(f32[648,32]{1,0:T(8,128)} %get-tuple-element.178), channel_id=1, source_target_pairs={{0,1},{1,2},{2,3},{3,4},{4,5},{5,6},{6,7},{7,8},{8,9},{9,10},{10,1... | collective-permute-start | bytes 248840 | tf_op jit(solution)/shard_map/ppermute | solution.py:31
  884.7 17.1 %collective-permute-start.12 = (f32[648,32]{1,0:T(8,128)S(1)}, f32[648,32]{1,0:T(8,128)S(1)}, u32[]{:S(2)}, u32[]{:S(2)}) collective-permute-start(f32[648,32]{1,0:T(8,128)S(1)} %get-tuple-element.167), channel_id=1, source_target_pairs={{0,1},{1,2},{2,3},{3,4},{4,5},{5,6},{6,7},{7,8},{8,9},{9,10},{10,1... | collective-permute-start | bytes 248840 | tf_op jit(solution)/shard_map/ppermute | solution.py:31
  888.1 18.4 %collective-permute-start.13 = (f32[648,32]{1,0:T(8,128)}, f32[648,32]{1,0:T(8,128)}, u32[]{:S(2)}, u32[]{:S(2)}) collective-permute-start(f32[648,32]{1,0:T(8,128)} %get-tuple-element.166), channel_id=1, source_target_pairs={{1,0},{2,1},{3,2},{4,3},{5,4},{6,5},{7,6},{8,7},{9,8},{10,9},{11,1... | collective-permute-start | bytes 248840 | tf_op jit(solution)/shard_map/ppermute | solution.py:32
  892.1 20.0 %collective-permute-start.11 = (f32[648,32]{1,0:T(8,128)}, f32[648,32]{1,0:T(8,128)}, u32[]{:S(2)}, u32[]{:S(2)}) collective-permute-start(f32[648,32]{1,0:T(8,128)} %get-tuple-element.177), channel_id=1, source_target_pairs={{1,0},{2,1},{3,2},{4,3},{5,4},{6,5},{7,6},{8,7},{9,8},{10,9},{11,1... | collective-permute-start | bytes 248840 | tf_op jit(solution)/shard_map/ppermute | solution.py:32
  894.2 18.0 %collective-permute-start.10 = (f32[648,32]{1,0:T(8,128)}, f32[648,32]{1,0:T(8,128)}, u32[]{:S(2)}, u32[]{:S(2)}) collective-permute-start(f32[648,32]{1,0:T(8,128)} %get-tuple-element.176), channel_id=1, source_target_pairs={{0,1},{1,2},{2,3},{3,4},{4,5},{5,6},{6,7},{7,8},{8,9},{9,10},{10,1... | collective-permute-start | bytes 248840 | tf_op jit(solution)/shard_map/ppermute | solution.py:31
  923.6 17.9 %collective-permute-start.16 = (f32[648,32]{1,0:T(8,128)S(1)}, f32[648,32]{1,0:T(8,128)S(1)}, u32[]{:S(2)}, u32[]{:S(2)}) collective-permute-start(f32[648,32]{1,0:T(8,128)S(1)} %get-tuple-element.165), channel_id=1, source_target_pairs={{0,1},{1,2},{2,3},{3,4},{4,5},{5,6},{6,7},{7,8},{8,9},{9,10},{10,1... | collective-permute-start | bytes 248840 | tf_op jit(solution)/shard_map/ppermute | solution.py:31
  925.5 20.7 %collective-permute-start.17 = (f32[648,32]{1,0:T(8,128)}, f32[648,32]{1,0:T(8,128)}, u32[]{:S(2)}, u32[]{:S(2)}) collective-permute-start(f32[648,32]{1,0:T(8,128)} %get-tuple-element.164), channel_id=1, source_target_pairs={{1,0},{2,1},{3,2},{4,3},{5,4},{6,5},{7,6},{8,7},{9,8},{10,9},{11,1... | collective-permute-start | bytes 248840 | tf_op jit(solution)/shard_map/ppermute | solution.py:32
  931.0 20.9 %collective-permute-start.15 = (f32[648,32]{1,0:T(8,128)}, f32[648,32]{1,0:T(8,128)}, u32[]{:S(2)}, u32[]{:S(2)}) collective-permute-start(f32[648,32]{1,0:T(8,128)} %get-tuple-element.175), channel_id=1, source_target_pairs={{1,0},{2,1},{3,2},{4,3},{5,4},{6,5},{7,6},{8,7},{9,8},{10,9},{11,1... | collective-permute-start | bytes 248840 | tf_op jit(solution)/shard_map/ppermute | solution.py:32
  933.1 18.8 %collective-permute-start.14 = (f32[648,32]{1,0:T(8,128)}, f32[648,32]{1,0:T(8,128)}, u32[]{:S(2)}, u32[]{:S(2)}) collective-permute-start(f32[648,32]{1,0:T(8,128)} %get-tuple-element.174), channel_id=1, source_target_pairs={{0,1},{1,2},{2,3},{3,4},{4,5},{5,6},{6,7},{7,8},{8,9},{9,10},{10,1... | collective-permute-start | bytes 248840 | tf_op jit(solution)/shard_map/ppermute | solution.py:31
  963.5 17.2 %collective-permute-start.20 = (f32[648,32]{1,0:T(8,128)S(1)}, f32[648,32]{1,0:T(8,128)S(1)}, u32[]{:S(2)}, u32[]{:S(2)}) collective-permute-start(f32[648,32]{1,0:T(8,128)S(1)} %get-tuple-element.163), channel_id=1, source_target_pairs={{0,1},{1,2},{2,3},{3,4},{4,5},{5,6},{6,7},{7,8},{8,9},{9,10},{10,1... | collective-permute-start | bytes 248840 | tf_op jit(solution)/shard_map/ppermute | solution.py:31
  965.4 20.0 %collective-permute-start.21 = (f32[648,32]{1,0:T(8,128)}, f32[648,32]{1,0:T(8,128)}, u32[]{:S(2)}, u32[]{:S(2)}) collective-permute-start(f32[648,32]{1,0:T(8,128)} %get-tuple-element.162), channel_id=1, source_target_pairs={{1,0},{2,1},{3,2},{4,3},{5,4},{6,5},{7,6},{8,7},{9,8},{10,9},{11,1... | collective-permute-start | bytes 248840 | tf_op jit(solution)/shard_map/ppermute | solution.py:32
  970.9 20.1 %collective-permute-start.19 = (f32[648,32]{1,0:T(8,128)}, f32[648,32]{1,0:T(8,128)}, u32[]{:S(2)}, u32[]{:S(2)}) collective-permute-start(f32[648,32]{1,0:T(8,128)} %get-tuple-element.173), channel_id=1, source_target_pairs={{1,0},{2,1},{3,2},{4,3},{5,4},{6,5},{7,6},{8,7},{9,8},{10,9},{11,1... | collective-permute-start | bytes 248840 | tf_op jit(solution)/shard_map/ppermute | solution.py:32
  973.0 18.1 %collective-permute-start.18 = (f32[648,32]{1,0:T(8,128)}, f32[648,32]{1,0:T(8,128)}, u32[]{:S(2)}, u32[]{:S(2)}) collective-permute-start(f32[648,32]{1,0:T(8,128)} %get-tuple-element.172), channel_id=1, source_target_pairs={{0,1},{1,2},{2,3},{3,4},{4,5},{5,6},{6,7},{7,8},{8,9},{9,10},{10,1... | collective-permute-start | bytes 248840 | tf_op jit(solution)/shard_map/ppermute | solution.py:31
  (8 other events, 1721.3 us)
where the time goes:
time: 1020 us; the launch traced here: 999 us
  local copies, waits for them, and re-layouts  400 us (39%)
  loops' own time  333 us (33%)
  blocking collectives  104 us (10%)
  starting transfers between devices  74.3 us (7%)
  matrix products  61.6 us (6%)
  other arithmetic  21.5 us (2%)
    another operation x1, loops' own time, entering(): return lax.fori_loop(0, place, one, state)  333 us
    dynamic_slice x508, local copies, waits for them, and re-layouts, one(): return combine(state, lax.dynamic_index_in_dim(gathered, turn, 0, False))  315 us
    all_gather x1, blocking collectives, entering(): gathered = lax.all_gather(part, axis)  104 us
    dot_general x45, matrix products, along(): jnp.einsum(forms[which], table, field, precision=lax.Precision.HIGHEST)  40.8 us
    ppermute x11, starting transfers between devices, extended_2(): after = lax.ppermute(initial, axis, down)  40.4 us
    ppermute x11, starting transfers between devices, extended_2(): before = lax.ppermute(last, axis, up)  34 us
    gather x4, local copies, waits for them, and re-layouts, shards(): rhs = jnp.take(load, order, axis=4)  20.6 us
  transfers between devices with their start and end apart: 22, of which 1 were waited for; matrix products, arithmetic and copies ran while one was open for 43% of the time, Pallas kernels for 0%

commit v1 on v0

v1 whole, which is shorter than its diff:
```python
import jax
import jax.numpy as jnp
from jax import lax
from jax.experimental import pallas as pl
from jax.experimental.pallas import tpu as pltpu
from jax.sharding import PartitionSpec as P

NODES = 6
COMPONENTS = 3
REACH = 32
SWEEPS = 2
DEGREE = 3
CELLS = 128
ROWS = COMPONENTS * NODES * NODES
QUADS = ROWS // 4
DENSE = 3 * QUADS
EDGE = 21
AXES = ("group", "rank")
THETA = (5.0 + 0.5) / 2.0
DELTA = (5.0 - 0.5) / 2.0
SIGMA = THETA / DELTA
F32, BF16, I32 = jnp.float32, jnp.bfloat16, jnp.int32


def iota(shape, dim):
    return lax.broadcasted_iota(I32, shape, dim)


def halves(x):
    high = x.astype(BF16)
    return high, (x - high.astype(F32)).astype(BF16)


def pack_kernel(load, order, degree, near, coupling, stiffness, lame, main, up, down, exclusive, padded):
    padded[:, NODES:8, :] = jnp.zeros((ROWS, 8 - NODES, CELLS), F32)
    padded[:, 0:NODES, :] = load[...]
    place = (iota((CELLS, CELLS), 0) == order[...]).astype(BF16)
    field = padded[...].reshape(ROWS * 8, CELLS)
    parts = jnp.concatenate(halves(field), axis=1)
    moved = jnp.dot(parts, jnp.concatenate([place, place], axis=0), preferred_element_type=F32)
    quads = moved.reshape(QUADS, 4, 8, CELLS)
    inner = iota((QUADS, 8, CELLS), 1) < NODES
    dense = [
        jnp.where(inner, quads[:, s], pltpu.roll(quads[:, 3], 6 - 2 * s, 1)) for s in range(3)
    ]
    degrees = jnp.broadcast_to(degree[...], (8, CELLS)).astype(F32).astype(BF16)
    cdeg = jnp.dot(degrees, place, preferred_element_type=F32)
    weight = (cdeg + 1.0) * (cdeg + 1.0) * (cdeg + 1.0)
    earlier = (iota((CELLS, CELLS), 0) < iota((CELLS, CELLS), 1)).astype(BF16)
    sums = jnp.dot(weight.astype(BF16), earlier, preferred_element_type=F32)
    exclusive[...] = sums[0:1].astype(I32)
    lane = iota((NB, CELLS), 1)
    offset = ((near[...] - lane + 64) & (CELLS - 1)) - 64
    rows = ((lane + offset) & (2 * CELLS - 1)).astype(F32)
    small0 = jnp.concatenate([rows, stiffness[...], lame[...]], axis=0)
    small1 = jnp.concatenate([coupling[...], cdeg[0:2]], axis=0)
    for s in range(3):
        main[s * QUADS : (s + 1) * QUADS] = dense[s]
    main[DENSE] = small0
    main[DENSE + 1] = small1
    lanes = iota((EDGE, 8, CELLS), 2)
    first, last = None, None
    for s in range(4):
        count = min(EDGE, DENSE - s * EDGE)
        piece = main[s * EDGE : s * EDGE + count]
        if count < EDGE:
            piece = jnp.concatenate([piece, jnp.zeros((EDGE - count, 8, CELLS), F32)], axis=0)
        head = piece if s == 0 else pltpu.roll(piece, REACH * s, 2)
        tail = piece if s == 3 else pltpu.roll(piece, REACH * s + REACH, 2)
        if s == 0:
            first, last = head, tail
        else:
            first = jnp.where(lanes >= REACH * s, head, first)
            last = jnp.where(lanes >= REACH * s, tail, last)
    down[0:EDGE] = first
    down[EDGE] = small0
    down[EDGE + 1] = small1
    up[0:EDGE] = last
    up[EDGE] = small0
    up[EDGE + 1] = small1


NB = 6
LEFT, OWN, RIGHT, OUTER, RIM = range(5)


def spread(dense):
    sub = iota((QUADS, 8, CELLS), 1)
    parts = [dense[s * QUADS : (s + 1) * QUADS] for s in range(3)]
    zero = jnp.zeros((QUADS, 8, CELLS), F32)
    tails = [pltpu.roll(parts[s], 2 * s + 2, 1) for s in range(3)]
    fourth = jnp.where(sub < 2, tails[0], jnp.where(sub < 4, tails[1], jnp.where(sub < 6, tails[2], zero)))
    return [jnp.where(sub < NODES, part, zero) for part in parts] + [fourth]


def smooth_kernel(own, left, right, outer_left, outer_right, out,
                  rhs, step, state_a, state_b, gain, stiff, table, low_table, couple, after_z, paired):
    low_lanes = lambda shape: iota(shape, len(shape) - 1) < 64

    for tile, source in ((LEFT, left), (OWN, own), (RIGHT, right)):
        for s, part in enumerate(spread(source[0:DENSE])):
            rhs[tile, :, s] = part
    pieces = []
    for s in range(4):
        lo = outer_right[0:EDGE] if s == 0 else pltpu.roll(outer_right[0:EDGE], CELLS - REACH * s, 2)
        hi = outer_left[0:EDGE] if s == 3 else pltpu.roll(outer_left[0:EDGE], 96 - REACH * s, 2)
        pieces.append(jnp.where(low_lanes((EDGE, 8, CELLS)), lo, hi))
    joined = jnp.concatenate(pieces, axis=0)
    for s, part in enumerate(spread(joined[0:DENSE])):
        rhs[OUTER, :, s] = part

    pick = low_lanes((8, CELLS))
    small = {
        LEFT: (left[DENSE], left[DENSE + 1]),
        OWN: (own[DENSE], own[DENSE + 1]),
        RIGHT: (right[DENSE], right[DENSE + 1]),
        OUTER: (
            jnp.where(pick, outer_right[EDGE], outer_left[EDGE]),
            jnp.where(pick, outer_right[EDGE + 1], outer_left[EDGE + 1]),
        ),
    }
    small[RIM] = tuple(jnp.where(pick, small[RIGHT][n], small[LEFT][n]) for n in range(2))
    sub = iota((8, CELLS), 0)
    for tile in range(5):
        shear, first_lame = small[tile][0][6:7], small[tile][0][7:8]
        diagonal = 1.0 / jnp.maximum(6.0 * shear + first_lame, 1e-6)
        cdeg = small[tile][1][6:7]
        for m in range(NODES):
            top = jnp.maximum(sub, m).astype(F32)
            gain[tile, m] = jnp.where(top <= cdeg, jnp.broadcast_to(diagonal, (8, CELLS)), 0.0)
        stiff[tile, 0] = jnp.broadcast_to(shear * (26.0 / 3.0), (8, CELLS))
        stiff[tile, 1] = jnp.broadcast_to(0.5 * first_lame - 20.0 * shear, (8, CELLS))
        stiff[tile, 2] = jnp.broadcast_to(0.5 * first_lame, (8, CELLS))

    def listed(tile, start, count):
        rows, weights = small[tile]
        place = (iota((count, CELLS), 0) + start).astype(F32)
        total = jnp.zeros((count, CELLS), F32)
        for k in range(NB):
            total = total + jnp.where(place == rows[k : k + 1], weights[k : k + 1], 0.0)
        return total

    inside = {tile: listed(tile, 0, CELLS) for tile in (LEFT, OWN, RIGHT)}
    across = {tile: listed(tile, CELLS, CELLS) for tile in (LEFT, OWN, RIGHT, OUTER)}
    wide = low_lanes((CELLS, CELLS))
    sides = {LEFT: (OWN, OUTER), OWN: (RIGHT, LEFT), RIGHT: (OUTER, OWN)}
    shear_of = {tile: jnp.broadcast_to(small[tile][0][6:7], (CELLS, CELLS)) for tile in range(4)}
    full = {}
    for tile, (after, before) in sides.items():
        top = inside[tile] + inside[tile].T
        bottom = across[tile] + jnp.where(wide, across[after], across[before]).T
        here = shear_of[tile]
        beside = jnp.where(wide, shear_of[after], shear_of[before])
        halved = []
        for values, other in ((top, here.T), (bottom, beside.T)):
            halved.append(values * (2.0 * here * other / jnp.maximum(here + other, 1e-6)))
        full[tile] = halved
    q = iota((CELLS, CELLS), 0)
    to_right = wide
    rim_top = jnp.where(
        to_right,
        jnp.where(q < 64, full[RIGHT][0], 0.0),
        jnp.where(q >= 64, full[LEFT][0], 0.0),
    )
    rim_bottom = jnp.where(
        to_right,
        jnp.where(q >= 96, full[RIGHT][1], jnp.where(q >= 64, full[RIGHT][0], 0.0)),
        jnp.where(q < 32, full[LEFT][1], jnp.where(q < 64, full[LEFT][0], 0.0)),
    )
    full[RIM] = [rim_top, rim_bottom]
    for slot, tile in enumerate((LEFT, OWN, RIGHT, RIM)):
        for half in range(2):
            high, low = halves(full[tile][half])
            table[slot, half * CELLS : (half + 1) * CELLS] = high
            table[slot, (2 + half) * CELLS : (3 + half) * CELLS] = high
            low_table[slot, half * CELLS : (half + 1) * CELLS] = low
    slot_of = {LEFT: 0, OWN: 1, RIGHT: 2, RIM: 3}

    edge = jnp.zeros((COMPONENTS, 6, 8, CELLS), F32)
    after_z[:, 0] = edge
    after_z[:, 7] = edge
    paired[:, 0] = edge
    paired[:, 7] = edge

    def first_step(tile):
        for r in range(QUADS):
            for s in range(4):
                row = 4 * r + s
                value = gain[tile, max(row // 6 % 6, row % 6)] * rhs[tile, r, s] * (1.0 / THETA)
                step[tile, r, s] = value
                state_a[tile, r, s] = value

    for tile in (LEFT, OWN, RIGHT, OUTER):
        first_step(tile)

    def apply(tile, source, beside, target, keep, scale, final=None):
        slot = slot_of[tile]
        here = source[tile].reshape(ROWS * 8, CELLS)
        there = beside().reshape(ROWS * 8, CELLS)
        (h1, l1), (h2, l2) = halves(here), halves(there)
        left_hand = jnp.concatenate([h1, h2, l1, l2], axis=1)
        result = jnp.dot(left_hand, table[slot], preferred_element_type=F32)
        result = result + jnp.dot(left_hand[:, : 2 * CELLS], low_table[slot], preferred_element_type=F32)
        couple[...] = result.reshape(COMPONENTS, 6, 6, 8, CELLS)
        for a in range(COMPONENTS):
            for i in range(6):
                u, y = [], []
                for j in range(6):
                    row = (a * 6 + i) * 6 + j
                    value = source[tile, row // 4, row % 4]
                    u.append(value)
                    y.append(value + 0.15 * (pltpu.roll(value, 1, 0) + pltpu.roll(value, 7, 0)))
                for j in range(6):
                    def beside_sum(values):
                        if j == 0:
                            return values[1]
                        if j == 5:
                            return values[4]
                        return values[j - 1] + values[j + 1]
                    z = y[j] + 0.15 * beside_sum(y)
                    x2 = u[j] + 0.15 * beside_sum(u)
                    after_z[a, i + 1, j] = z
                    paired[a, i + 1, j] = y[j] + x2
        k0, k1, k2 = stiff[tile, 0], stiff[tile, 1], stiff[tile, 2]
        for i in range(6):
            for j in range(6):
                ms, vs = [], []
                for a in range(COMPONENTS):
                    z = after_z[a, i + 1, j]
                    ms.append(z + 0.15 * (after_z[a, i, j] + after_z[a, i + 2, j]))
                    vs.append(z + paired[a, i + 1, j] + 0.15 * (paired[a, i, j] + paired[a, i + 2, j]))
                mixed = k2 * (ms[0] + ms[1] + ms[2])
                g = gain[tile, max(i, j)] * scale
                for a in range(COMPONENTS):
                    row = (a * 6 + i) * 6 + j
                    r, s = row // 4, row % 4
                    resid = (rhs[tile, r, s] - mixed) + (couple[a, i, j] - k0 * vs[a] - k1 * ms[a])
                    delta = g * resid
                    if keep is not None:
                        delta = delta + keep * step[tile, r, s]
                    value = source[tile, r, s] + delta
                    if final is None:
                        step[tile, r, s] = delta
                        target[tile, r, s] = value
                    else:
                        final[row] = value[0:NODES]

    rho0 = 1.0 / SIGMA
    rho1 = 1.0 / (2.0 * SIGMA - rho0)
    rho2 = 1.0 / (2.0 * SIGMA - rho1)
    first = (rho1 * rho0, 2.0 * rho1 / DELTA)
    second = (rho2 * rho1, 2.0 * rho2 / DELTA)
    low = low_lanes((QUADS, 4, 8, CELLS))
    join = lambda x, y: jnp.where(low, x, y)

    for source, target, (keep, scale) in ((state_a, state_b, first), (state_b, state_a, second)):
        apply(LEFT, source, lambda: join(source[OWN], state_a[OUTER]), target, keep, scale)
        apply(OWN, source, lambda: join(source[RIGHT], source[LEFT]), target, keep, scale)
        apply(RIGHT, source, lambda: join(state_a[OUTER], source[OWN]), target, keep, scale)
    state_a[RIM] = join(state_a[RIGHT], state_a[LEFT])
    rhs[RIM] = join(rhs[RIGHT], rhs[LEFT])
    lanes = iota((QUADS, 4, 8, CELLS), 3)
    ends = (lanes < 32) | (lanes >= 96)
    for source, target, (keep, scale) in (
        (state_a, state_b, (None, 1.0 / THETA)),
        (state_b, state_a, first),
    ):
        apply(OWN, source, lambda: source[RIM], target, keep, scale)
        apply(RIM, source, lambda: jnp.where(ends, source[OWN], join(state_a[LEFT], state_a[RIGHT])), target, keep, scale)
    apply(OWN, state_a, lambda: state_a[RIM], None, second[0], second[1], out)


def shards(degree, curve_order, neighbours, coupling, stiffness, lame, load):
    devices = lax.axis_size(AXES)
    groups, ranks = lax.axis_size("group"), lax.axis_size("rank")
    group, rank = lax.axis_index("group"), lax.axis_index("rank")
    vmem = pl.BlockSpec(memory_space=pltpu.VMEM)
    row = lambda x: x.reshape(1, CELLS)
    packed = pl.pallas_call(
        pack_kernel,
        out_shape=(
            jax.ShapeDtypeStruct((DENSE + 2, 8, CELLS), F32),
            jax.ShapeDtypeStruct((EDGE + 2, 8, CELLS), F32),
            jax.ShapeDtypeStruct((EDGE + 2, 8, CELLS), F32),
            jax.ShapeDtypeStruct((1, CELLS), I32),
        ),
        in_specs=[vmem] * 7,
        out_specs=[vmem] * 4,
        scratch_shapes=[pltpu.VMEM((ROWS, 8, CELLS), F32)],
        compiler_params=pltpu.CompilerParams(vmem_limit_bytes=32 * 1024 * 1024),
        name="pack",
    )(load.reshape(ROWS, NODES, CELLS), curve_order, row(degree), neighbours, coupling, row(stiffness), row(lame))
    main, up, down, exclusive = packed

    def shifted(array, by):
        pairs = [(i, i + by) for i in range(max(0, -by), min(devices, devices - by))]
        return lax.ppermute(array, AXES, pairs)

    left, right = shifted(main, 1), shifted(main, -1)
    outer_left, outer_right = shifted(up, 2), shifted(down, -2)

    local_total = jnp.sum((degree + 1) ** 3)
    by_rank = jnp.where(jnp.arange(ranks, dtype=I32) == rank, local_total, 0)
    by_rank = lax.psum(by_rank, "rank")
    in_group = jnp.sum(jnp.where(jnp.arange(ranks, dtype=I32) < rank, by_rank, 0))
    by_group = jnp.where(jnp.arange(groups, dtype=I32) == group, jnp.sum(by_rank), 0)
    by_group = lax.psum(by_group, "group")
    before = in_group + jnp.sum(jnp.where(jnp.arange(groups, dtype=I32) < group, by_group, 0))
    share = (jnp.sum(by_group) + devices - 1) // devices
    owner = (before + exclusive.reshape(CELLS)) // share

    block = (QUADS, 4, 8, CELLS)
    smoothed = pl.pallas_call(
        smooth_kernel,
        out_shape=jax.ShapeDtypeStruct((ROWS, NODES, CELLS), F32),
        in_specs=[vmem] * 5,
        out_specs=vmem,
        scratch_shapes=[
            pltpu.VMEM((5, *block), F32),
            pltpu.VMEM((5, *block), F32),
            pltpu.VMEM((5, *block), F32),
            pltpu.VMEM((5, *block), F32),
            pltpu.VMEM((5, NODES, 8, CELLS), F32),
            pltpu.VMEM((5, 3, 8, CELLS), F32),
            pltpu.VMEM((4, 4 * CELLS, CELLS), BF16),
            pltpu.VMEM((4, 2 * CELLS, CELLS), BF16),
            pltpu.VMEM((COMPONENTS, 6, 6, 8, CELLS), F32),
            pltpu.VMEM((COMPONENTS, 8, 6, 8, CELLS), F32),
            pltpu.VMEM((COMPONENTS, 8, 6, 8, CELLS), F32),
        ],
        compiler_params=pltpu.CompilerParams(vmem_limit_bytes=48 * 1024 * 1024),
        name="smooth",
    )(main, left, right, outer_left, outer_right)
    return owner, smoothed.reshape(COMPONENTS, NODES, NODES, NODES, CELLS)


def solution(mesh):
    return jax.shard_map(
        shards,
        mesh=mesh,
        in_specs=(
            P(AXES),
            P(AXES, None),
            P(None, AXES),
            P(None, AXES),
            P(AXES),
            P(AXES),
            P(None, None, None, None, AXES),
        ),
        out_specs=(P(AXES), P(None, None, None, None, AXES)),
        check_vma=False,
    )
```

time: 1020 us -> 78.4 us (0.08)
  the two profiles are of different devices: /device:TPU:487 before, /device:TPU:8 now
where the time goes in v1:
time: 78.4 us; the launch traced here: 78 us
  blocking collectives  46 us (59%)
  starting transfers between devices  13.4 us (17%)
  Pallas kernels  9.52 us (12%)
  other arithmetic  3.92 us (5%)
  between operations  2.76 us (4%)
  local copies, waits for them, and re-layouts  2.38 us (3%)
    psum x1, blocking collectives, shards(): by_rank = lax.psum(by_rank, 'rank')  32 us
    psum x1, blocking collectives, shards(): by_group = lax.psum(by_group, 'group')  14 us
    ppermute x4, starting transfers between devices, shifted(): return lax.ppermute(array, AXES, pairs)  13.4 us
    pallas_call x1, Pallas kernels, shards(): pl.pallas_call(smooth_kernel, out_shape=jax.ShapeDtypeStruct((ROWS, NODES...  9.09 us
    unnamed x14, local copies, waits for them, and re-layouts  2.38 us
  transfers between devices with their start and end apart: 4, of which 0 were waited for; matrix products, arithmetic and copies ran while one was open for 5% of the time, Pallas kernels for 0%

profile of v1, /device:TPU:8, one launch (start us, length us, event | category | flops | bytes accessed | tf_op | source)
XLA Modules:
  0.0 78.0 jit_solution(1908073771461990518)
XLA Ops:
  0.6 0.0 copy-start.1
  0.7 0.6 copy-done.1
  1.3 0.0 copy-done.4
  1.3 0.0 copy-done.5
  1.4 1.0 %copy-done = f32[3,6,6,6,128]{4,3,2,1,0:T(8,128)S(1)} copy-done((f32[3,6,6,6,128]{4,3,2,1,0:T(8,128)S(1)}, f32[3,6,6,6,128]{4,3,2,1,0:T(8,128)}, u32[]{:S(2)}) %copy-start) | copy-done | bytes 331800
  2.4 0.7 copy-done.2
  3.1 0.4 pack.1
  3.5 7.7 %collective-permute-start.1 = (f32[83,8,128]{2,1,0:T(8,128)S(1)}, f32[83,8,128]{2,1,0:T(8,128)S(1)}, u32[]{:S(2)}, u32[]{:S(2)}) collective-permute-start(f32[83,8,128]{2,1,0:T(8,128)S(1)} %get-tuple-element.7.own), channel_id=1, source_target_pairs={{1,0},{2,1},{3,2},{4,3},{5,4},{6,5},{7,6},{8,7},{9,8},{10,9},{11,1... | collective-permute-start | bytes 1019912 | tf_op jit(solution)/shard_map/ppermute | solution.py:297
  11.2 1.9 %collective-permute-start = (f32[83,8,128]{2,1,0:T(8,128)S(1)}, f32[83,8,128]{2,1,0:T(8,128)S(1)}, u32[]{:S(2)}, u32[]{:S(2)}) collective-permute-start(f32[83,8,128]{2,1,0:T(8,128)S(1)} %get-tuple-element.7.own), channel_id=1, source_target_pairs={{0,1},{1,2},{2,3},{3,4},{4,5},{5,6},{6,7},{7,8},{8,9},{9,10},{10,1... | collective-permute-start | bytes 1019912 | tf_op jit(solution)/shard_map/ppermute | solution.py:297
  13.1 2.5 %collective-permute-start.2 = (f32[23,8,128]{2,1,0:T(8,128)S(1)}, f32[23,8,128]{2,1,0:T(8,128)S(1)}, u32[]{:S(2)}, u32[]{:S(2)}) collective-permute-start(f32[23,8,128]{2,1,0:T(8,128)S(1)} %get-tuple-element.8), channel_id=1, source_target_pairs={{0,2},{1,3},{2,4},{3,5},{4,6},{5,7},{6,8},{7,9},{8,10},{9,11},{10,... | collective-permute-start | bytes 282632 | tf_op jit(solution)/shard_map/ppermute | solution.py:297
  15.7 0.6 fusion
  16.3 0.6 compare_select_fusion.2
  16.9 32.0 %psum.14 = s32[64]{0:T(128)S(1)} all-reduce(s32[64]{0:T(128)S(1)} %compare_select_fusion.2), channel_id=1, replica_groups=mesh['group'=8,'rank'=64] {'rank'}, use_global_device_ids=true, to_apply=%region_1.2 | all-reduce | flops 64 | bytes 512 | tf_op jit(solution)/shard_map/psum | solution.py:304
  48.9 0.6 fusion.1
  49.5 0.6 compare_select_fusion
  50.2 1.3 %collective-permute-start.3 = (f32[23,8,128]{2,1,0:T(8,128)S(1)}, f32[23,8,128]{2,1,0:T(8,128)S(1)}, u32[]{:S(2)}, u32[]{:S(2)}) collective-permute-start(f32[23,8,128]{2,1,0:T(8,128)S(1)} %get-tuple-element.9), channel_id=1, source_target_pairs={{2,0},{3,1},{4,2},{5,3},{6,4},{7,5},{8,6},{9,7},{10,8},{11,9},{12,... | collective-permute-start | bytes 282632 | tf_op jit(solution)/shard_map/ppermute | solution.py:297
  51.5 14.0 %psum.15 = s32[8]{0:T(128)S(1)} all-reduce(s32[8]{0:T(128)S(1)} %compare_select_fusion), channel_id=1, replica_groups=mesh['group'=8,'rank'=64] {'group'}, use_global_device_ids=true, to_apply=%region_4.5 | all-reduce | flops 8 | bytes 64 | tf_op jit(solution)/shard_map/psum | solution.py:307
  65.5 0.7 fusion.2
  68.3 0.6 bitcast_select_fusion
  68.9 0.0 collective-permute-done.2.outer_left
  68.9 0.0 collective-permute-done.3.outer_right
  68.9 0.0 collective-permute-done.1.right
  68.9 0.0 collective-permute-done.left
  68.9 9.1 %smooth.1 = f32[108,6,128]{2,1,0:T(8,128)} custom-call(f32[83,8,128]{2,1,0:T(8,128)S(1)} %get-tuple-element.7.own, f32[83,8,128]{2,1,0:T(8,128)S(1)} %collective-permute-done.left, f32[83,8,128]{2,1,0:T(8,128)S(1)} %collective-permute-done.1.right, f32[23,8,128]{2,1,0:T(8,128)S(1)} %collective-permute-done.2.outer_left, ...), custom_call_target="tpu_custom_call" | custom-call | tf_op jit(solution)/shard_map/smooth/pallas_call | solution.py:313
  (8 shorter events, 0.0 us)
Async XLA Ops:
  0.6 0.7 copy-start.1
  0.6 0.7 copy-start.6
  0.7 0.7 copy-start.3
  0.7 0.7 copy-start.4
  0.7 0.7 copy-start.5
  1.4 1.0 %copy-start = (f32[3,6,6,6,128]{4,3,2,1,0:T(8,128)S(1)}, f32[3,6,6,6,128]{4,3,2,1,0:T(8,128)}, u32[]{:S(2)}) copy-start(f32[3,6,6,6,128]{4,3,2,1,0:T(8,128)} %param.13) | copy-start | bytes 995332
  2.4 0.7 copy-start.2
  3.5 65.4 %collective-permute-start.1 = (f32[83,8,128]{2,1,0:T(8,128)S(1)}, f32[83,8,128]{2,1,0:T(8,128)S(1)}, u32[]{:S(2)}, u32[]{:S(2)}) collective-permute-start(f32[83,8,128]{2,1,0:T(8,128)S(1)} %get-tuple-element.7.own), channel_id=1, source_target_pairs={{1,0},{2,1},{3,2},{4,3},{5,4},{6,5},{7,6},{8,7},{9,8},{10,9},{11,1... | collective-permute-start | bytes 1019912 | tf_op jit(solution)/shard_map/ppermute | solution.py:297
  11.2 57.7 %collective-permute-start = (f32[83,8,128]{2,1,0:T(8,128)S(1)}, f32[83,8,128]{2,1,0:T(8,128)S(1)}, u32[]{:S(2)}, u32[]{:S(2)}) collective-permute-start(f32[83,8,128]{2,1,0:T(8,128)S(1)} %get-tuple-element.7.own), channel_id=1, source_target_pairs={{0,1},{1,2},{2,3},{3,4},{4,5},{5,6},{6,7},{7,8},{8,9},{9,10},{10,1... | collective-permute-start | bytes 1019912 | tf_op jit(solution)/shard_map/ppermute | solution.py:297
  13.1 55.8 %collective-permute-start.2 = (f32[23,8,128]{2,1,0:T(8,128)S(1)}, f32[23,8,128]{2,1,0:T(8,128)S(1)}, u32[]{:S(2)}, u32[]{:S(2)}) collective-permute-start(f32[23,8,128]{2,1,0:T(8,128)S(1)} %get-tuple-element.8), channel_id=1, source_target_pairs={{0,2},{1,3},{2,4},{3,5},{4,6},{5,7},{6,8},{7,9},{8,10},{9,11},{10,... | collective-permute-start | bytes 282632 | tf_op jit(solution)/shard_map/ppermute | solution.py:297
  50.2 18.7 %collective-permute-start.3 = (f32[23,8,128]{2,1,0:T(8,128)S(1)}, f32[23,8,128]{2,1,0:T(8,128)S(1)}, u32[]{:S(2)}, u32[]{:S(2)}) collective-permute-start(f32[23,8,128]{2,1,0:T(8,128)S(1)} %get-tuple-element.9), channel_id=1, source_target_pairs={{2,0},{3,1},{4,2},{5,3},{6,4},{7,5},{8,6},{9,7},{10,8},{11,9},{12,... | collective-permute-start | bytes 282632 | tf_op jit(solution)/shard_map/ppermute | solution.py:297

commit v2 on v1

--- a/solution.py
+++ b/solution.py
@@ -31,8 +31,15 @@
     return high, (x - high.astype(F32)).astype(BF16)
 
 
-def pack_kernel(load, order, degree, near, coupling, stiffness, lame, main, up, down, exclusive, padded):
+def pack_kernel(*refs):
+    sources, (main, up, down, exclusive, weights, padded), held, arrived = refs[:7], refs[7:13], refs[13:20], refs[20]
+    copies = [pltpu.make_async_copy(a, b, arrived.at[n]) for n, (a, b) in enumerate(zip(sources, held))]
+    for copy in copies:
+        copy.start()
     padded[:, NODES:8, :] = jnp.zeros((ROWS, 8 - NODES, CELLS), F32)
+    for copy in copies:
+        copy.wait()
+    load, order, degree, near, coupling, stiffness, lame = held
     padded[:, 0:NODES, :] = load[...]
     place = (iota((CELLS, CELLS), 0) == order[...]).astype(BF16)
     field = padded[...].reshape(ROWS * 8, CELLS)
@@ -49,6 +56,9 @@
     earlier = (iota((CELLS, CELLS), 0) < iota((CELLS, CELLS), 1)).astype(BF16)
     sums = jnp.dot(weight.astype(BF16), earlier, preferred_element_type=F32)
     exclusive[...] = sums[0:1].astype(I32)
+    group = lax.axis_index("group")
+    segment = jnp.sum(weight[0:1], axis=1, keepdims=True).astype(I32)
+    weights[...] = jnp.where(iota((1, CELLS), 1) == group, segment, 0)
     lane = iota((NB, CELLS), 1)
     offset = ((near[...] - lane + 64) & (CELLS - 1)) - 64
     rows = ((lane + offset) & (2 * CELLS - 1)).astype(F32)
@@ -270,12 +280,27 @@
     apply(OWN, state_a, lambda: state_a[RIM], None, second[0], second[1], out)
 
 
+def owner_kernel(totals, exclusive, owner):
+    group, rank = lax.axis_index("group"), lax.axis_index("rank")
+    devices = lax.axis_size(AXES)
+    values = totals[...].astype(F32)
+    rows, columns = iota(values.shape, 0), iota(values.shape, 1)
+    earlier = (columns < group) | ((columns == group) & (rows < rank))
+    whole = lambda x: jnp.sum(jnp.sum(x, axis=0, keepdims=True), axis=1, keepdims=True)
+    before = whole(jnp.where(earlier, values, 0.0)) + exclusive[...].astype(F32)
+    share = jnp.floor((whole(values) + (devices - 1.0)) * (1.0 / devices))
+    place = jnp.floor(before * (1.0 / share))
+    left = before - place * share
+    place = place + jnp.where(left < 0.0, -1.0, jnp.where(left >= share, 1.0, 0.0))
+    owner[...] = place.astype(I32)
+
+
 def shards(degree, curve_order, neighbours, coupling, stiffness, lame, load):
     devices = lax.axis_size(AXES)
-    groups, ranks = lax.axis_size("group"), lax.axis_size("rank")
-    group, rank = lax.axis_index("group"), lax.axis_index("rank")
+    ranks = lax.axis_size("rank")
     vmem = pl.BlockSpec(memory_space=pltpu.VMEM)
     row = lambda x: x.reshape(1, CELLS)
+    arguments = (load.reshape(ROWS, NODES, CELLS), curve_order, row(degree), neighbours, coupling, row(stiffness), row(lame))
     packed = pl.pallas_call(
         pack_kernel,
         out_shape=(
@@ -283,14 +308,21 @@
             jax.ShapeDtypeStruct((EDGE + 2, 8, CELLS), F32),
             jax.ShapeDtypeStruct((EDGE + 2, 8, CELLS), F32),
             jax.ShapeDtypeStruct((1, CELLS), I32),
+            jax.ShapeDtypeStruct((1, CELLS), I32),
         ),
-        in_specs=[vmem] * 7,
-        out_specs=[vmem] * 4,
-        scratch_shapes=[pltpu.VMEM((ROWS, 8, CELLS), F32)],
+        in_specs=[pl.BlockSpec(memory_space=pltpu.HBM)] * 7,
+        out_specs=[vmem] * 5,
+        scratch_shapes=[
+            pltpu.VMEM((ROWS, 8, CELLS), F32),
+            *[pltpu.VMEM(x.shape, x.dtype) for x in arguments],
+            pltpu.SemaphoreType.DMA((7,)),
+        ],
         compiler_params=pltpu.CompilerParams(vmem_limit_bytes=32 * 1024 * 1024),
         name="pack",
-    )(load.reshape(ROWS, NODES, CELLS), curve_order, row(degree), neighbours, coupling, row(stiffness), row(lame))
-    main, up, down, exclusive = packed
+    )(*arguments)
+    main, up, down, exclusive, weights = packed
+    weights = lax.psum(weights, "group")
+    main, up, down, weights = lax.optimization_barrier((main, up, down, weights))
 
     def shifted(array, by):
         pairs = [(i, i + by) for i in range(max(0, -by), min(devices, devices - by))]
@@ -299,15 +331,7 @@
     left, right = shifted(main, 1), shifted(main, -1)
     outer_left, outer_right = shifted(up, 2), shifted(down, -2)
 
-    local_total = jnp.sum((degree + 1) ** 3)
-    by_rank = jnp.where(jnp.arange(ranks, dtype=I32) == rank, local_total, 0)
-    by_rank = lax.psum(by_rank, "rank")
-    in_group = jnp.sum(jnp.where(jnp.arange(ranks, dtype=I32) < rank, by_rank, 0))
-    by_group = jnp.where(jnp.arange(groups, dtype=I32) == group, jnp.sum(by_rank), 0)
-    by_group = lax.psum(by_group, "group")
-    before = in_group + jnp.sum(jnp.where(jnp.arange(groups, dtype=I32) < group, by_group, 0))
-    share = (jnp.sum(by_group) + devices - 1) // devices
-    owner = (before + exclusive.reshape(CELLS)) // share
+    totals = lax.all_to_all(jnp.broadcast_to(weights, (ranks, CELLS)), "rank", 0, 0, tiled=True)
 
     block = (QUADS, 4, 8, CELLS)
     smoothed = pl.pallas_call(
@@ -315,6 +339,7 @@
         out_shape=jax.ShapeDtypeStruct((ROWS, NODES, CELLS), F32),
         in_specs=[vmem] * 5,
         out_specs=vmem,
+        cost_estimate=pl.CostEstimate(flops=7 * 10**9, bytes_accessed=10**6, transcendentals=0),
         scratch_shapes=[
             pltpu.VMEM((5, *block), F32),
             pltpu.VMEM((5, *block), F32),
@@ -331,7 +356,15 @@
         compiler_params=pltpu.CompilerParams(vmem_limit_bytes=48 * 1024 * 1024),
         name="smooth",
     )(main, left, right, outer_left, outer_right)
-    return owner, smoothed.reshape(COMPONENTS, NODES, NODES, NODES, CELLS)
+    totals, smoothed = lax.optimization_barrier((totals, smoothed))
+    owner = pl.pallas_call(
+        owner_kernel,
+        out_shape=jax.ShapeDtypeStruct((1, CELLS), I32),
+        in_specs=[pl.BlockSpec(), vmem],
+        out_specs=vmem,
+        name="owner",
+    )(totals.reshape(ranks, CELLS), exclusive)
+    return owner.reshape(CELLS), smoothed.reshape(COMPONENTS, NODES, NODES, NODES, CELLS)
 
 
 def solution(mesh):

time: 78.4 us -> 65 us (0.83)
  blocking collectives: 46 us -> 9.22 us
  starting transfers between devices: 13.4 us -> 34.7 us
  waiting for transfers between devices: 0.01 us -> 4.64 us
  other arithmetic: 3.92 us -> 0 us
  between operations: 2.76 us -> 0.77 us
  local copies, waits for them, and re-layouts: 2.38 us -> 4.17 us
  Pallas kernels: 9.52 us -> 11 us
    psum x2 -> x1, blocking collectives: 46 us -> 9.22 us  [shards(): weights = lax.psum(weights, 'group')]
    all_to_all x0 -> x1, starting transfers between devices: none -> 23.4 us  [shards(): lax.all_to_all(jnp.broadcast_to(weights, (ranks, CELLS)), 'rank', 0, 0, t...]
    all_to_all x0 -> x1, waiting for transfers between devices: none -> 4.63 us  [shards(): lax.all_to_all(jnp.broadcast_to(weights, (ranks, CELLS)), 'rank', 0, 0, t...]
    ppermute x4, starting transfers between devices: 13.4 us -> 11.3 us  [shifted(): return lax.ppermute(array, AXES, pairs)]
    reduce_sum x3 -> x0, other arithmetic: 1.99 us -> none  [the longest x1 0.72 us: shards(): jnp.sum(jnp.where(jnp.arange(groups, dtype=I32) < group, by_group, 0))]
    select_n x3 -> x0, other arithmetic: 1.93 us -> none  [the longest x1 0.65 us: shards(): by_rank = jnp.where(jnp.arange(ranks, dtype=I32) == rank, local_total, 0)]
    pallas_call x0 -> x1, Pallas kernels: none -> 1.38 us  [shards(): pl.pallas_call(owner_kernel, out_shape=jax.ShapeDtypeStruct((1, CELLS), I...]
    unnamed x14 -> x18, local copies, waits for them, and re-layouts: 2.38 us -> 3.55 us
  transfers between devices with their start and end apart: 4 -> 5, of which waited for: 0 -> 1; matrix products, arithmetic and copies ran while one was open for 5% -> 1% of each run, Pallas kernels for 0% -> 14%
where the time goes in v2:
time: 65 us; the launch traced here: 64.5 us
  starting transfers between devices  34.7 us (53%)
  Pallas kernels  11 us (17%)
  blocking collectives  9.22 us (14%)
  waiting for transfers between devices  4.64 us (7%)
  local copies, waits for them, and re-layouts  4.17 us (6%)
  between operations  0.77 us (1%)
    all_to_all x1, starting transfers between devices, shards(): lax.all_to_all(jnp.broadcast_to(weights, (ranks, CELLS)), 'rank', 0, 0, t...  23.4 us
    ppermute x4, starting transfers between devices, shifted(): return lax.ppermute(array, AXES, pairs)  11.3 us
    psum x1, blocking collectives, shards(): weights = lax.psum(weights, 'group')  9.22 us
    pallas_call x1, Pallas kernels, shards(): pl.pallas_call(smooth_kernel, out_shape=jax.ShapeDtypeStruct((ROWS, NODES...  9.11 us
    all_to_all x1, waiting for transfers between devices, shards(): lax.all_to_all(jnp.broadcast_to(weights, (ranks, CELLS)), 'rank', 0, 0, t...  4.63 us
    unnamed x18, local copies, waits for them, and re-layouts  3.55 us
    pallas_call x1, Pallas kernels, shards(): pl.pallas_call(owner_kernel, out_shape=jax.ShapeDtypeStruct((1, CELLS), I...  1.38 us
  transfers between devices with their start and end apart: 5, of which 1 were waited for; matrix products, arithmetic and copies ran while one was open for 1% of the time, Pallas kernels for 14%

profile of v2, /device:TPU:8, one launch (start us, length us, event | category | flops | bytes accessed | tf_op | source)
XLA Modules:
  0.0 64.5 jit_solution(14650639022305803661)
XLA Ops:
  0.6 0.0 copy-start.1
  0.6 0.0 copy-start.6
  0.7 0.6 copy-done.1
  1.3 0.0 copy-done.4
  1.3 0.0 copy-done.5
  1.4 1.0 %copy-done = f32[3,6,6,6,128]{4,3,2,1,0:T(8,128)S(1)} copy-done((f32[3,6,6,6,128]{4,3,2,1,0:T(8,128)S(1)}, f32[3,6,6,6,128]{4,3,2,1,0:T(8,128)}, u32[]{:S(2)}) %copy-start) | copy-done | bytes 331800
  2.4 0.7 %copy-done.2 = f32[6,128]{1,0:T(8,128)S(1)} copy-done((f32[6,128]{1,0:T(8,128)S(1)}, f32[6,128]{1,0:T(8,128)}, u32[]{:S(2)}) %copy-start.2) | copy-done | bytes 3096
  3.1 0.6 pack.1
  3.6 0.6 copy-done.7
  4.2 9.2 %psum.7 = s32[1,128]{1,0:T(1,128)S(1)} all-reduce(s32[1,128]{1,0:T(1,128)S(1)} %get-tuple-element.16), channel_id=1, replica_groups=mesh['group'=8,'rank'=64] {'group'}, use_global_device_ids=true, to_apply=%region_0.0 | all-reduce | flops 128 | bytes 1024 | tf_op jit(solution)/shard_map/psum | solution.py:324
  13.4 3.5 %collective-permute-start = (f32[83,8,128]{2,1,0:T(8,128)S(1)}, f32[83,8,128]{2,1,0:T(8,128)S(1)}, u32[]{:S(2)}, u32[]{:S(2)}) collective-permute-start(f32[83,8,128]{2,1,0:T(8,128)S(1)} %get-tuple-element.18.own), channel_id=1, source_target_pairs={{0,1},{1,2},{2,3},{3,4},{4,5},{5,6},{6,7},{7,8},{8,9},{9,10},{10,1... | collective-permute-start | bytes 1019912 | tf_op jit(solution)/shard_map/ppermute | solution.py:329
  16.9 2.4 %collective-permute-start.1 = (f32[83,8,128]{2,1,0:T(8,128)S(1)}, f32[83,8,128]{2,1,0:T(8,128)S(1)}, u32[]{:S(2)}, u32[]{:S(2)}) collective-permute-start(f32[83,8,128]{2,1,0:T(8,128)S(1)} %get-tuple-element.18.own), channel_id=1, source_target_pairs={{1,0},{2,1},{3,2},{4,3},{5,4},{6,5},{7,6},{8,7},{9,8},{10,9},{11,1... | collective-permute-start | bytes 1019912 | tf_op jit(solution)/shard_map/ppermute | solution.py:329
  19.3 4.2 %collective-permute-start.2 = (f32[23,8,128]{2,1,0:T(8,128)S(1)}, f32[23,8,128]{2,1,0:T(8,128)S(1)}, u32[]{:S(2)}, u32[]{:S(2)}) collective-permute-start(f32[23,8,128]{2,1,0:T(8,128)S(1)} %get-tuple-element.19), channel_id=1, source_target_pairs={{0,2},{1,3},{2,4},{3,5},{4,6},{5,7},{6,8},{7,9},{8,10},{9,11},{10,... | collective-permute-start | bytes 282632 | tf_op jit(solution)/shard_map/ppermute | solution.py:329
  23.5 1.3 %collective-permute-start.3 = (f32[23,8,128]{2,1,0:T(8,128)S(1)}, f32[23,8,128]{2,1,0:T(8,128)S(1)}, u32[]{:S(2)}, u32[]{:S(2)}) collective-permute-start(f32[23,8,128]{2,1,0:T(8,128)S(1)} %get-tuple-element.20), channel_id=1, source_target_pairs={{2,0},{3,1},{4,2},{5,3},{6,4},{7,5},{8,6},{9,7},{10,8},{11,9},{12,... | collective-permute-start | bytes 282632 | tf_op jit(solution)/shard_map/ppermute | solution.py:329
  24.8 0.6 broadcast_in_dim.2
  25.4 23.4 %all-to-all-start = ((s32[64,1,128]{2,1,0:T(1,128)}), s32[64,1,128]{2,1,0:T(1,128)S(1)}, u32[]{:S(2)}, u32[]{:S(2)}) async-start(s32[64,1,128]{2,1,0:T(1,128)} %broadcast_in_dim.2), calls=%async_computation | async-start | bytes 65536 | tf_op jit(solution)/shard_map/all_to_all | solution.py:334
  48.8 0.0 collective-permute-done.2.outer_left
  48.8 0.0 collective-permute-done.3.outer_right
  48.8 0.0 collective-permute-done.left
  48.8 0.0 collective-permute-done.1.right
  48.8 9.1 %smooth.1 = f32[108,6,128]{2,1,0:T(8,128)} custom-call(f32[83,8,128]{2,1,0:T(8,128)S(1)} %get-tuple-element.18.own, f32[83,8,128]{2,1,0:T(8,128)S(1)} %collective-permute-done.left, f32[83,8,128]{2,1,0:T(8,128)S(1)} %collective-permute-done.1.right, f32[23,8,128]{2,1,0:T(8,128)S(1)} %collective-permute-done.2.outer_left, ...), custom_call_target="tpu_custom_call" | custom-call | flops 7000000000 | bytes 1000000 | tf_op jit(solution)/shard_map/smooth/pallas_call | solution.py:337
  57.9 4.6 %all-to-all-done = s32[64,1,128]{2,1,0:T(1,128)S(1)} async-done(((s32[64,1,128]{2,1,0:T(1,128)}), s32[64,1,128]{2,1,0:T(1,128)S(1)}, u32[]{:S(2)}, u32[]{:S(2)}) %all-to-all-start) | async-done | bytes 32800 | tf_op jit(solution)/shard_map/all_to_all | solution.py:334
  62.6 0.6 copy-done.8
  63.2 1.4 %owner.1 = s32[1,128]{1,0:T(1,128)} custom-call(s32[64,128]{1,0:T(8,128)} %bitcast.12, s32[1,128]{1,0:T(1,128)} %copy-done.7), custom_call_target="tpu_custom_call" | custom-call | tf_op jit(solution)/shard_map/owner/pallas_call | solution.py:360
  (9 shorter events, 0.0 us)
Async XLA Ops:
  0.6 0.7 %copy-start.1 = (s32[6,128]{1,0:T(8,128)S(1)}, s32[6,128]{1,0:T(8,128)}, u32[]{:S(2)}) copy-start(s32[6,128]{1,0:T(8,128)} %refs_3_.1) | copy-start | bytes 9220
  0.6 0.7 %copy-start.6 = (f32[128]{0:T(128)S(1)}, f32[128]{0:T(128)}, u32[]{:S(2)}) copy-start(f32[128]{0:T(128)} %param.12) | copy-start | bytes 1540
  0.7 0.7 %copy-start.3 = (s32[1,128]{1,0:T(1,128)S(1)}, s32[1,128]{1,0:T(1,128)}, u32[]{:S(2)}) copy-start(s32[1,128]{1,0:T(1,128)} %refs_1_.1) | copy-start | bytes 1540
  0.7 0.7 %copy-start.4 = (s32[128]{0:T(128)S(1)}, s32[128]{0:T(128)}, u32[]{:S(2)}) copy-start(s32[128]{0:T(128)} %param.7) | copy-start | bytes 1540
  0.7 0.7 %copy-start.5 = (f32[128]{0:T(128)S(1)}, f32[128]{0:T(128)}, u32[]{:S(2)}) copy-start(f32[128]{0:T(128)} %param.11) | copy-start | bytes 1540
  1.4 1.0 %copy-start = (f32[3,6,6,6,128]{4,3,2,1,0:T(8,128)S(1)}, f32[3,6,6,6,128]{4,3,2,1,0:T(8,128)}, u32[]{:S(2)}) copy-start(f32[3,6,6,6,128]{4,3,2,1,0:T(8,128)} %param.13) | copy-start | bytes 995332
  2.4 0.7 %copy-start.2 = (f32[6,128]{1,0:T(8,128)S(1)}, f32[6,128]{1,0:T(8,128)}, u32[]{:S(2)}) copy-start(f32[6,128]{1,0:T(8,128)} %refs_4_.1) | copy-start | bytes 9220
  3.6 0.6 copy-start.7
  13.4 35.4 %collective-permute-start = (f32[83,8,128]{2,1,0:T(8,128)S(1)}, f32[83,8,128]{2,1,0:T(8,128)S(1)}, u32[]{:S(2)}, u32[]{:S(2)}) collective-permute-start(f32[83,8,128]{2,1,0:T(8,128)S(1)} %get-tuple-element.18.own), channel_id=1, source_target_pairs={{0,1},{1,2},{2,3},{3,4},{4,5},{5,6},{6,7},{7,8},{8,9},{9,10},{10,1... | collective-permute-start | bytes 1019912 | tf_op jit(solution)/shard_map/ppermute | solution.py:329
  16.9 31.9 %collective-permute-start.1 = (f32[83,8,128]{2,1,0:T(8,128)S(1)}, f32[83,8,128]{2,1,0:T(8,128)S(1)}, u32[]{:S(2)}, u32[]{:S(2)}) collective-permute-start(f32[83,8,128]{2,1,0:T(8,128)S(1)} %get-tuple-element.18.own), channel_id=1, source_target_pairs={{1,0},{2,1},{3,2},{4,3},{5,4},{6,5},{7,6},{8,7},{9,8},{10,9},{11,1... | collective-permute-start | bytes 1019912 | tf_op jit(solution)/shard_map/ppermute | solution.py:329
  19.3 29.5 %collective-permute-start.2 = (f32[23,8,128]{2,1,0:T(8,128)S(1)}, f32[23,8,128]{2,1,0:T(8,128)S(1)}, u32[]{:S(2)}, u32[]{:S(2)}) collective-permute-start(f32[23,8,128]{2,1,0:T(8,128)S(1)} %get-tuple-element.19), channel_id=1, source_target_pairs={{0,2},{1,3},{2,4},{3,5},{4,6},{5,7},{6,8},{7,9},{8,10},{9,11},{10,... | collective-permute-start | bytes 282632 | tf_op jit(solution)/shard_map/ppermute | solution.py:329
  23.5 25.3 %collective-permute-start.3 = (f32[23,8,128]{2,1,0:T(8,128)S(1)}, f32[23,8,128]{2,1,0:T(8,128)S(1)}, u32[]{:S(2)}, u32[]{:S(2)}) collective-permute-start(f32[23,8,128]{2,1,0:T(8,128)S(1)} %get-tuple-element.20), channel_id=1, source_target_pairs={{2,0},{3,1},{4,2},{5,3},{6,4},{7,5},{8,6},{9,7},{10,8},{11,9},{12,... | collective-permute-start | bytes 282632 | tf_op jit(solution)/shard_map/ppermute | solution.py:329
  25.4 37.2 %all-to-all-start = ((s32[64,1,128]{2,1,0:T(1,128)}), s32[64,1,128]{2,1,0:T(1,128)S(1)}, u32[]{:S(2)}, u32[]{:S(2)}) async-start(s32[64,1,128]{2,1,0:T(1,128)} %broadcast_in_dim.2), calls=%async_computation | async-start | bytes 65536 | tf_op jit(solution)/shard_map/all_to_all | solution.py:334
  62.6 0.6 copy-start.8

commit v3 on v2

--- a/solution.py
+++ b/solution.py
@@ -104,7 +104,7 @@
 
 
 def smooth_kernel(own, left, right, outer_left, outer_right, out,
-                  rhs, step, state_a, state_b, gain, stiff, table, low_table, couple, after_z, paired):
+                  results, sent, rhs, step, state_a, state_b, gain, stiff, table, couple, after_z, paired):
     low_lanes = lambda shape: iota(shape, len(shape) - 1) < 64
 
     for tile, source in ((LEFT, left), (OWN, own), (RIGHT, right)):
@@ -183,7 +183,7 @@
             high, low = halves(full[tile][half])
             table[slot, half * CELLS : (half + 1) * CELLS] = high
             table[slot, (2 + half) * CELLS : (3 + half) * CELLS] = high
-            low_table[slot, half * CELLS : (half + 1) * CELLS] = low
+            table[slot, (4 + half) * CELLS : (5 + half) * CELLS] = low
     slot_of = {LEFT: 0, OWN: 1, RIGHT: 2, RIM: 3}
 
     edge = jnp.zeros((COMPONENTS, 6, 8, CELLS), F32)
@@ -205,14 +205,14 @@
 
     def apply(tile, source, beside, target, keep, scale, final=None):
         slot = slot_of[tile]
-        here = source[tile].reshape(ROWS * 8, CELLS)
-        there = beside().reshape(ROWS * 8, CELLS)
-        (h1, l1), (h2, l2) = halves(here), halves(there)
-        left_hand = jnp.concatenate([h1, h2, l1, l2], axis=1)
-        result = jnp.dot(left_hand, table[slot], preferred_element_type=F32)
-        result = result + jnp.dot(left_hand[:, : 2 * CELLS], low_table[slot], preferred_element_type=F32)
-        couple[...] = result.reshape(COMPONENTS, 6, 6, 8, CELLS)
+        part = ROWS // 4 // COMPONENTS
         for a in range(COMPONENTS):
+            here = source[tile, a * part : (a + 1) * part].reshape(part * 32, CELLS)
+            there = beside(slice(a * part, (a + 1) * part)).reshape(part * 32, CELLS)
+            (h1, l1), (h2, l2) = halves(here), halves(there)
+            left_hand = jnp.concatenate([h1, h2, l1, l2, h1, h2], axis=1)
+            result = jnp.dot(left_hand, table[slot], preferred_element_type=F32)
+            couple[a] = result.reshape(6, 6, 8, CELLS)
             for i in range(6):
                 u, y = [], []
                 for j in range(6):
@@ -253,31 +253,38 @@
                         step[tile, r, s] = delta
                         target[tile, r, s] = value
                     else:
-                        final[row] = value[0:NODES]
+                        results[row] = value[0:NODES]
+            if final is not None:
+                for a in range(COMPONENTS):
+                    rows = pl.ds((a * 6 + i) * 6, 6)
+                    pltpu.make_async_copy(results.at[rows], final.at[rows], sent.at[a * 6 + i]).start()
+        if final is not None:
+            for n in range(COMPONENTS * 6):
+                rows = pl.ds(n * 6, 6)
+                pltpu.make_async_copy(results.at[rows], final.at[rows], sent.at[n]).wait()
 
     rho0 = 1.0 / SIGMA
     rho1 = 1.0 / (2.0 * SIGMA - rho0)
     rho2 = 1.0 / (2.0 * SIGMA - rho1)
     first = (rho1 * rho0, 2.0 * rho1 / DELTA)
     second = (rho2 * rho1, 2.0 * rho2 / DELTA)
-    low = low_lanes((QUADS, 4, 8, CELLS))
-    join = lambda x, y: jnp.where(low, x, y)
+    join = lambda x, y: jnp.where(low_lanes(x.shape), x, y)
 
     for source, target, (keep, scale) in ((state_a, state_b, first), (state_b, state_a, second)):
-        apply(LEFT, source, lambda: join(source[OWN], state_a[OUTER]), target, keep, scale)
-        apply(OWN, source, lambda: join(source[RIGHT], source[LEFT]), target, keep, scale)
-        apply(RIGHT, source, lambda: join(state_a[OUTER], source[OWN]), target, keep, scale)
+        apply(LEFT, source, lambda p: join(source[OWN, p], state_a[OUTER, p]), target, keep, scale)
+        apply(OWN, source, lambda p: join(source[RIGHT, p], source[LEFT, p]), target, keep, scale)
+        apply(RIGHT, source, lambda p: join(state_a[OUTER, p], source[OWN, p]), target, keep, scale)
     state_a[RIM] = join(state_a[RIGHT], state_a[LEFT])
     rhs[RIM] = join(rhs[RIGHT], rhs[LEFT])
-    lanes = iota((QUADS, 4, 8, CELLS), 3)
+    lanes = iota((QUADS // COMPONENTS, 4, 8, CELLS), 3)
     ends = (lanes < 32) | (lanes >= 96)
     for source, target, (keep, scale) in (
         (state_a, state_b, (None, 1.0 / THETA)),
         (state_b, state_a, first),
     ):
-        apply(OWN, source, lambda: source[RIM], target, keep, scale)
-        apply(RIM, source, lambda: jnp.where(ends, source[OWN], join(state_a[LEFT], state_a[RIGHT])), target, keep, scale)
-    apply(OWN, state_a, lambda: state_a[RIM], None, second[0], second[1], out)
+        apply(OWN, source, lambda p: source[RIM, p], target, keep, scale)
+        apply(RIM, source, lambda p: jnp.where(ends, source[OWN, p], join(state_a[LEFT, p], state_a[RIGHT, p])), target, keep, scale)
+    apply(OWN, state_a, lambda p: state_a[RIM, p], None, second[0], second[1], out)
 
 
 def owner_kernel(totals, exclusive, owner):
@@ -301,6 +308,7 @@
     vmem = pl.BlockSpec(memory_space=pltpu.VMEM)
     row = lambda x: x.reshape(1, CELLS)
     arguments = (load.reshape(ROWS, NODES, CELLS), curve_order, row(degree), neighbours, coupling, row(stiffness), row(lame))
+    arguments = tuple(pltpu.with_memory_space_constraint(x, pltpu.HBM) for x in arguments)
     packed = pl.pallas_call(
         pack_kernel,
         out_shape=(
@@ -338,17 +346,18 @@
         smooth_kernel,
         out_shape=jax.ShapeDtypeStruct((ROWS, NODES, CELLS), F32),
         in_specs=[vmem] * 5,
-        out_specs=vmem,
+        out_specs=pl.BlockSpec(memory_space=pltpu.HBM),
         cost_estimate=pl.CostEstimate(flops=7 * 10**9, bytes_accessed=10**6, transcendentals=0),
         scratch_shapes=[
+            pltpu.VMEM((ROWS, NODES, CELLS), F32),
+            pltpu.SemaphoreType.DMA((COMPONENTS * 6,)),
             pltpu.VMEM((5, *block), F32),
             pltpu.VMEM((5, *block), F32),
             pltpu.VMEM((5, *block), F32),
             pltpu.VMEM((5, *block), F32),
             pltpu.VMEM((5, NODES, 8, CELLS), F32),
             pltpu.VMEM((5, 3, 8, CELLS), F32),
-            pltpu.VMEM((4, 4 * CELLS, CELLS), BF16),
-            pltpu.VMEM((4, 2 * CELLS, CELLS), BF16),
+            pltpu.VMEM((4, 6 * CELLS, CELLS), BF16),
             pltpu.VMEM((COMPONENTS, 6, 6, 8, CELLS), F32),
             pltpu.VMEM((COMPONENTS, 8, 6, 8, CELLS), F32),
             pltpu.VMEM((COMPONENTS, 8, 6, 8, CELLS), F32),

time: 65 us -> 63.2 us (0.972)
  local copies, waits for them, and re-layouts: 4.17 us -> 1.81 us
    unnamed x18 -> x4, local copies, waits for them, and re-layouts: 3.55 us -> 1.18 us
    pallas_call x1, Pallas kernels: 0.55 us -> 1.45 us  [shards(): pl.pallas_call(pack_kernel, out_shape=(jax.ShapeDtypeStruct((DENSE + 2, 8...]
    pallas_call x1, Pallas kernels: 9.11 us -> 8.45 us  [shards(): pl.pallas_call(smooth_kernel, out_shape=jax.ShapeDtypeStruct((ROWS, NODES...]
  transfers between devices with their start and end apart: 5 -> 5, of which waited for: 1 -> 1; matrix products, arithmetic and copies ran while one was open for 1% -> 1% of each run, Pallas kernels for 14% -> 13%
where the time goes in v3:
time: 63.2 us; the launch traced here: 62.9 us
  starting transfers between devices  34.7 us (55%)
  Pallas kernels  11.3 us (18%)
  blocking collectives  9.22 us (15%)
  waiting for transfers between devices  5.13 us (8%)
  local copies, waits for them, and re-layouts  1.81 us (3%)
  between operations  0.73 us (1%)
    all_to_all x1, starting transfers between devices, shards(): lax.all_to_all(jnp.broadcast_to(weights, (ranks, CELLS)), 'rank', 0, 0, t...  23.4 us
    ppermute x4, starting transfers between devices, shifted(): return lax.ppermute(array, AXES, pairs)  11.3 us
    psum x1, blocking collectives, shards(): weights = lax.psum(weights, 'group')  9.22 us
    pallas_call x1, Pallas kernels, shards(): pl.pallas_call(smooth_kernel, out_shape=jax.ShapeDtypeStruct((ROWS, NODES...  8.45 us
    all_to_all x1, waiting for transfers between devices, shards(): lax.all_to_all(jnp.broadcast_to(weights, (ranks, CELLS)), 'rank', 0, 0, t...  5.12 us
    pallas_call x1, Pallas kernels, shards(): pl.pallas_call(pack_kernel, out_shape=(jax.ShapeDtypeStruct((DENSE + 2, 8...  1.45 us
    pallas_call x1, Pallas kernels, shards(): pl.pallas_call(owner_kernel, out_shape=jax.ShapeDtypeStruct((1, CELLS), I...  1.38 us
  transfers between devices with their start and end apart: 5, of which 1 were waited for; matrix products, arithmetic and copies ran while one was open for 1% of the time, Pallas kernels for 13%

profile of v3, /device:TPU:8, one launch (start us, length us, event | category | flops | bytes accessed | tf_op | source)
XLA Modules:
  0.0 62.9 jit_solution(3761004667181949480)
XLA Ops:
  0.6 1.5 %pack.1 = (f32[83,8,128]{2,1,0:T(8,128)S(1)}, f32[23,8,128]{2,1,0:T(8,128)S(1)}, f32[23,8,128]{2,1,0:T(8,128)S(1)}, s32[1,128]{1,0:T(1,128)S(1)}, s32[1,128]{1,0:T(1,128)S(1)}) custom-call(f32[108,6,128]{2,1,0:T(8,128)} %bitcast.8, s32[1,128]{1,0:T(1,128)} %refs_1_.1, s32[1,128]{1,0:T(1,128)} %bitcast.10, s32[6,128]{1,0:T(8,128)} %refs_3_.1, ...), custom_call_target="tpu_custom_call" | custom-call | tf_op jit(solution)/shard_map/pack/pallas_call | solution.py:312
  2.1 0.0 copy-start
  2.1 0.6 copy-done
  2.7 9.2 %psum.7 = s32[1,128]{1,0:T(1,128)S(1)} all-reduce(s32[1,128]{1,0:T(1,128)S(1)} %get-tuple-element.16), channel_id=1, replica_groups=mesh['group'=8,'rank'=64] {'group'}, use_global_device_ids=true, to_apply=%region_0.0 | all-reduce | flops 128 | bytes 1024 | tf_op jit(solution)/shard_map/psum | solution.py:332
  11.9 3.5 %collective-permute-start = (f32[83,8,128]{2,1,0:T(8,128)S(1)}, f32[83,8,128]{2,1,0:T(8,128)S(1)}, u32[]{:S(2)}, u32[]{:S(2)}) collective-permute-start(f32[83,8,128]{2,1,0:T(8,128)S(1)} %get-tuple-element.18.own), channel_id=1, source_target_pairs={{0,1},{1,2},{2,3},{3,4},{4,5},{5,6},{6,7},{7,8},{8,9},{9,10},{10,1... | collective-permute-start | bytes 1019912 | tf_op jit(solution)/shard_map/ppermute | solution.py:337
  15.4 2.4 %collective-permute-start.1 = (f32[83,8,128]{2,1,0:T(8,128)S(1)}, f32[83,8,128]{2,1,0:T(8,128)S(1)}, u32[]{:S(2)}, u32[]{:S(2)}) collective-permute-start(f32[83,8,128]{2,1,0:T(8,128)S(1)} %get-tuple-element.18.own), channel_id=1, source_target_pairs={{1,0},{2,1},{3,2},{4,3},{5,4},{6,5},{7,6},{8,7},{9,8},{10,9},{11,1... | collective-permute-start | bytes 1019912 | tf_op jit(solution)/shard_map/ppermute | solution.py:337
  17.8 4.2 %collective-permute-start.2 = (f32[23,8,128]{2,1,0:T(8,128)S(1)}, f32[23,8,128]{2,1,0:T(8,128)S(1)}, u32[]{:S(2)}, u32[]{:S(2)}) collective-permute-start(f32[23,8,128]{2,1,0:T(8,128)S(1)} %get-tuple-element.19), channel_id=1, source_target_pairs={{0,2},{1,3},{2,4},{3,5},{4,6},{5,7},{6,8},{7,9},{8,10},{9,11},{10,... | collective-permute-start | bytes 282632 | tf_op jit(solution)/shard_map/ppermute | solution.py:337
  22.0 1.3 %collective-permute-start.3 = (f32[23,8,128]{2,1,0:T(8,128)S(1)}, f32[23,8,128]{2,1,0:T(8,128)S(1)}, u32[]{:S(2)}, u32[]{:S(2)}) collective-permute-start(f32[23,8,128]{2,1,0:T(8,128)S(1)} %get-tuple-element.20), channel_id=1, source_target_pairs={{2,0},{3,1},{4,2},{5,3},{6,4},{7,5},{8,6},{9,7},{10,8},{11,9},{12,... | collective-permute-start | bytes 282632 | tf_op jit(solution)/shard_map/ppermute | solution.py:337
  23.3 0.6 %broadcast_in_dim.2 = s32[64,1,128]{2,1,0:T(1,128)} broadcast(s32[128]{0:T(128)S(1)} %bitcast.13), dimensions={2} | broadcast | bytes 33280 | tf_op jit(solution)/shard_map/broadcast_in_dim | solution.py:342
  23.9 23.4 %all-to-all-start = ((s32[64,1,128]{2,1,0:T(1,128)}), s32[64,1,128]{2,1,0:T(1,128)S(1)}, u32[]{:S(2)}, u32[]{:S(2)}) async-start(s32[64,1,128]{2,1,0:T(1,128)} %broadcast_in_dim.2), calls=%async_computation | async-start | bytes 65536 | tf_op jit(solution)/shard_map/all_to_all | solution.py:342
  47.3 0.0 collective-permute-done.2.outer_left
  47.3 0.0 collective-permute-done.3.outer_right
  47.3 0.0 collective-permute-done.left
  47.3 0.0 collective-permute-done.1.right
  47.3 8.4 %smooth.1 = f32[108,6,128]{2,1,0:T(8,128)} custom-call(f32[83,8,128]{2,1,0:T(8,128)S(1)} %get-tuple-element.18.own, f32[83,8,128]{2,1,0:T(8,128)S(1)} %collective-permute-done.left, f32[83,8,128]{2,1,0:T(8,128)S(1)} %collective-permute-done.1.right, f32[23,8,128]{2,1,0:T(8,128)S(1)} %collective-permute-done.2.outer_left, ...), custom_call_target="tpu_custom_call" | custom-call | flops 7000000000 | bytes 1000000 | tf_op jit(solution)/shard_map/smooth/pallas_call | solution.py:345
  55.8 5.1 %all-to-all-done = s32[64,1,128]{2,1,0:T(1,128)S(1)} async-done(((s32[64,1,128]{2,1,0:T(1,128)}), s32[64,1,128]{2,1,0:T(1,128)S(1)}, u32[]{:S(2)}, u32[]{:S(2)}) %all-to-all-start) | async-done | bytes 32800 | tf_op jit(solution)/shard_map/all_to_all | solution.py:342
  60.9 0.0 copy-start.1
  60.9 0.6 copy-done.1
  61.5 1.4 %owner.1 = s32[1,128]{1,0:T(1,128)} custom-call(s32[64,128]{1,0:T(8,128)} %bitcast.9, s32[1,128]{1,0:T(1,128)} %copy-done), custom_call_target="tpu_custom_call" | custom-call | tf_op jit(solution)/shard_map/owner/pallas_call | solution.py:369
Async XLA Ops:
  2.1 0.6 copy-start
  11.9 35.4 %collective-permute-start = (f32[83,8,128]{2,1,0:T(8,128)S(1)}, f32[83,8,128]{2,1,0:T(8,128)S(1)}, u32[]{:S(2)}, u32[]{:S(2)}) collective-permute-start(f32[83,8,128]{2,1,0:T(8,128)S(1)} %get-tuple-element.18.own), channel_id=1, source_target_pairs={{0,1},{1,2},{2,3},{3,4},{4,5},{5,6},{6,7},{7,8},{8,9},{9,10},{10,1... | collective-permute-start | bytes 1019912 | tf_op jit(solution)/shard_map/ppermute | solution.py:337
  15.4 31.9 %collective-permute-start.1 = (f32[83,8,128]{2,1,0:T(8,128)S(1)}, f32[83,8,128]{2,1,0:T(8,128)S(1)}, u32[]{:S(2)}, u32[]{:S(2)}) collective-permute-start(f32[83,8,128]{2,1,0:T(8,128)S(1)} %get-tuple-element.18.own), channel_id=1, source_target_pairs={{1,0},{2,1},{3,2},{4,3},{5,4},{6,5},{7,6},{8,7},{9,8},{10,9},{11,1... | collective-permute-start | bytes 1019912 | tf_op jit(solution)/shard_map/ppermute | solution.py:337
  17.8 29.5 %collective-permute-start.2 = (f32[23,8,128]{2,1,0:T(8,128)S(1)}, f32[23,8,128]{2,1,0:T(8,128)S(1)}, u32[]{:S(2)}, u32[]{:S(2)}) collective-permute-start(f32[23,8,128]{2,1,0:T(8,128)S(1)} %get-tuple-element.19), channel_id=1, source_target_pairs={{0,2},{1,3},{2,4},{3,5},{4,6},{5,7},{6,8},{7,9},{8,10},{9,11},{10,... | collective-permute-start | bytes 282632 | tf_op jit(solution)/shard_map/ppermute | solution.py:337
  22.0 25.3 %collective-permute-start.3 = (f32[23,8,128]{2,1,0:T(8,128)S(1)}, f32[23,8,128]{2,1,0:T(8,128)S(1)}, u32[]{:S(2)}, u32[]{:S(2)}) collective-permute-start(f32[23,8,128]{2,1,0:T(8,128)S(1)} %get-tuple-element.20), channel_id=1, source_target_pairs={{2,0},{3,1},{4,2},{5,3},{6,4},{7,5},{8,6},{9,7},{10,8},{11,9},{12,... | collective-permute-start | bytes 282632 | tf_op jit(solution)/shard_map/ppermute | solution.py:337
  23.9 37.0 %all-to-all-start = ((s32[64,1,128]{2,1,0:T(1,128)}), s32[64,1,128]{2,1,0:T(1,128)S(1)}, u32[]{:S(2)}, u32[]{:S(2)}) async-start(s32[64,1,128]{2,1,0:T(1,128)} %broadcast_in_dim.2), calls=%async_computation | async-start | bytes 65536 | tf_op jit(solution)/shard_map/all_to_all | solution.py:342
  60.9 0.6 copy-start.1

commit v4 on v3

--- a/solution.py
+++ b/solution.py
@@ -347,7 +347,7 @@
         out_shape=jax.ShapeDtypeStruct((ROWS, NODES, CELLS), F32),
         in_specs=[vmem] * 5,
         out_specs=pl.BlockSpec(memory_space=pltpu.HBM),
-        cost_estimate=pl.CostEstimate(flops=7 * 10**9, bytes_accessed=10**6, transcendentals=0),
+        cost_estimate=pl.CostEstimate(flops=10**6, bytes_accessed=10**3, transcendentals=0),
         scratch_shapes=[
             pltpu.VMEM((ROWS, NODES, CELLS), F32),
             pltpu.SemaphoreType.DMA((COMPONENTS * 6,)),

time: 63.2 us -> 62.6 us (level)
  the two profiles are of different devices: /device:TPU:8 before, /device:TPU:120 now
where the time goes in v4:
time: 62.6 us; the launch traced here: 62.2 us
  starting transfers between devices  31.1 us (50%)
  Pallas kernels  11.3 us (18%)
  blocking collectives  9.22 us (15%)
  waiting for transfers between devices  8.16 us (13%)
  local copies, waits for them, and re-layouts  1.8 us (3%)
  between operations  0.72 us (1%)
    all_to_all x1, starting transfers between devices, shards(): lax.all_to_all(jnp.broadcast_to(weights, (ranks, CELLS)), 'rank', 0, 0, t...  17.1 us
    ppermute x4, starting transfers between devices, shifted(): return lax.ppermute(array, AXES, pairs)  14 us
    psum x1, blocking collectives, shards(): weights = lax.psum(weights, 'group')  9.22 us
    pallas_call x1, Pallas kernels, shards(): pl.pallas_call(smooth_kernel, out_shape=jax.ShapeDtypeStruct((ROWS, NODES...  8.45 us
    ppermute x4, waiting for transfers between devices, shifted(): return lax.ppermute(array, AXES, pairs)  8.16 us
    pallas_call x1, Pallas kernels, shards(): pl.pallas_call(pack_kernel, out_shape=(jax.ShapeDtypeStruct((DENSE + 2, 8...  1.45 us
    pallas_call x1, Pallas kernels, shards(): pl.pallas_call(owner_kernel, out_shape=jax.ShapeDtypeStruct((1, CELLS), I...  1.38 us
  transfers between devices with their start and end apart: 5, of which 2 were waited for; matrix products, arithmetic and copies ran while one was open for 1% of the time, Pallas kernels for 14%

profile of v4, /device:TPU:120, one launch (start us, length us, event | category | flops | bytes accessed | tf_op | source)
XLA Modules:
  0.0 62.2 jit_solution(4859545472487357684)
XLA Ops:
  0.6 1.5 %pack.1 = (f32[83,8,128]{2,1,0:T(8,128)S(1)}, f32[23,8,128]{2,1,0:T(8,128)S(1)}, f32[23,8,128]{2,1,0:T(8,128)S(1)}, s32[1,128]{1,0:T(1,128)S(1)}, s32[1,128]{1,0:T(1,128)S(1)}) custom-call(f32[108,6,128]{2,1,0:T(8,128)} %bitcast.8, s32[1,128]{1,0:T(1,128)} %refs_1_.1, s32[1,128]{1,0:T(1,128)} %bitcast.11, s32[6,128]{1,0:T(8,128)} %refs_3_.1, ...), custom_call_target="tpu_custom_call" | custom-call | tf_op jit(solution)/shard_map/pack/pallas_call | solution.py:312
  2.1 0.0 copy-start
  2.1 0.6 copy-done
  2.7 9.2 %psum.7 = s32[1,128]{1,0:T(1,128)S(1)} all-reduce(s32[1,128]{1,0:T(1,128)S(1)} %get-tuple-element.16), channel_id=1, replica_groups=mesh['group'=8,'rank'=64] {'group'}, use_global_device_ids=true, to_apply=%region_0.0 | all-reduce | flops 128 | bytes 1024 | tf_op jit(solution)/shard_map/psum | solution.py:332
  11.9 4.7 %collective-permute-start = (f32[83,8,128]{2,1,0:T(8,128)S(1)}, f32[83,8,128]{2,1,0:T(8,128)S(1)}, u32[]{:S(2)}, u32[]{:S(2)}) collective-permute-start(f32[83,8,128]{2,1,0:T(8,128)S(1)} %get-tuple-element.18.own), channel_id=1, source_target_pairs={{0,1},{1,2},{2,3},{3,4},{4,5},{5,6},{6,7},{7,8},{8,9},{9,10},{10,1... | collective-permute-start | bytes 1019912 | tf_op jit(solution)/shard_map/ppermute | solution.py:337
  16.6 1.9 %collective-permute-start.1 = (f32[83,8,128]{2,1,0:T(8,128)S(1)}, f32[83,8,128]{2,1,0:T(8,128)S(1)}, u32[]{:S(2)}, u32[]{:S(2)}) collective-permute-start(f32[83,8,128]{2,1,0:T(8,128)S(1)} %get-tuple-element.18.own), channel_id=1, source_target_pairs={{1,0},{2,1},{3,2},{4,3},{5,4},{6,5},{7,6},{8,7},{9,8},{10,9},{11,1... | collective-permute-start | bytes 1019912 | tf_op jit(solution)/shard_map/ppermute | solution.py:337
  18.5 0.6 %broadcast_in_dim.2 = s32[64,1,128]{2,1,0:T(1,128)} broadcast(s32[128]{0:T(128)S(1)} %bitcast.15), dimensions={2} | broadcast | bytes 33280 | tf_op jit(solution)/shard_map/broadcast_in_dim | solution.py:342
  19.1 17.1 %all-to-all-start = ((s32[64,1,128]{2,1,0:T(1,128)}), s32[64,1,128]{2,1,0:T(1,128)S(1)}, u32[]{:S(2)}, u32[]{:S(2)}) async-start(s32[64,1,128]{2,1,0:T(1,128)} %broadcast_in_dim.2), calls=%async_computation | async-start | bytes 65536 | tf_op jit(solution)/shard_map/all_to_all | solution.py:342
  36.2 5.5 %collective-permute-start.2 = (f32[23,8,128]{2,1,0:T(8,128)S(1)}, f32[23,8,128]{2,1,0:T(8,128)S(1)}, u32[]{:S(2)}, u32[]{:S(2)}) collective-permute-start(f32[23,8,128]{2,1,0:T(8,128)S(1)} %get-tuple-element.19), channel_id=1, source_target_pairs={{0,2},{1,3},{2,4},{3,5},{4,6},{5,7},{6,8},{7,9},{8,10},{9,11},{10,... | collective-permute-start | bytes 282632 | tf_op jit(solution)/shard_map/ppermute | solution.py:337
  41.7 1.9 %collective-permute-start.3 = (f32[23,8,128]{2,1,0:T(8,128)S(1)}, f32[23,8,128]{2,1,0:T(8,128)S(1)}, u32[]{:S(2)}, u32[]{:S(2)}) collective-permute-start(f32[23,8,128]{2,1,0:T(8,128)S(1)} %get-tuple-element.20), channel_id=1, source_target_pairs={{2,0},{3,1},{4,2},{5,3},{6,4},{7,5},{8,6},{9,7},{10,8},{11,9},{12,... | collective-permute-start | bytes 282632 | tf_op jit(solution)/shard_map/ppermute | solution.py:337
  43.6 0.6 collective-permute-done.2.outer_left
  44.2 7.6 %collective-permute-done.3.outer_right = f32[23,8,128]{2,1,0:T(8,128)S(1)} collective-permute-done((f32[23,8,128]{2,1,0:T(8,128)S(1)}, f32[23,8,128]{2,1,0:T(8,128)S(1)}, u32[]{:S(2)}, u32[]{:S(2)}) %collective-permute-start.3) | collective-permute-done | bytes 94240 | tf_op jit(solution)/shard_map/ppermute | solution.py:337
  51.8 0.0 collective-permute-done.left
  51.8 0.0 collective-permute-done.1.right
  51.8 8.5 %smooth.1 = f32[108,6,128]{2,1,0:T(8,128)} custom-call(f32[83,8,128]{2,1,0:T(8,128)S(1)} %get-tuple-element.18.own, f32[83,8,128]{2,1,0:T(8,128)S(1)} %collective-permute-done.left, f32[83,8,128]{2,1,0:T(8,128)S(1)} %collective-permute-done.1.right, f32[23,8,128]{2,1,0:T(8,128)S(1)} %collective-permute-done.2.outer_left, ...), custom_call_target="tpu_custom_call" | custom-call | flops 1000000 | bytes 1000 | tf_op jit(solution)/shard_map/smooth/pallas_call | solution.py:345
  60.2 0.0 all-to-all-done
  60.3 0.0 copy-start.1
  60.3 0.6 copy-done.1
  60.9 1.4 %owner.1 = s32[1,128]{1,0:T(1,128)} custom-call(s32[64,128]{1,0:T(8,128)} %bitcast.10, s32[1,128]{1,0:T(1,128)} %copy-done), custom_call_target="tpu_custom_call" | custom-call | tf_op jit(solution)/shard_map/owner/pallas_call | solution.py:369
Async XLA Ops:
  2.1 0.6 copy-start
  11.9 39.9 %collective-permute-start = (f32[83,8,128]{2,1,0:T(8,128)S(1)}, f32[83,8,128]{2,1,0:T(8,128)S(1)}, u32[]{:S(2)}, u32[]{:S(2)}) collective-permute-start(f32[83,8,128]{2,1,0:T(8,128)S(1)} %get-tuple-element.18.own), channel_id=1, source_target_pairs={{0,1},{1,2},{2,3},{3,4},{4,5},{5,6},{6,7},{7,8},{8,9},{9,10},{10,1... | collective-permute-start | bytes 1019912 | tf_op jit(solution)/shard_map/ppermute | solution.py:337
  16.6 35.2 %collective-permute-start.1 = (f32[83,8,128]{2,1,0:T(8,128)S(1)}, f32[83,8,128]{2,1,0:T(8,128)S(1)}, u32[]{:S(2)}, u32[]{:S(2)}) collective-permute-start(f32[83,8,128]{2,1,0:T(8,128)S(1)} %get-tuple-element.18.own), channel_id=1, source_target_pairs={{1,0},{2,1},{3,2},{4,3},{5,4},{6,5},{7,6},{8,7},{9,8},{10,9},{11,1... | collective-permute-start | bytes 1019912 | tf_op jit(solution)/shard_map/ppermute | solution.py:337
  19.1 41.1 %all-to-all-start = ((s32[64,1,128]{2,1,0:T(1,128)}), s32[64,1,128]{2,1,0:T(1,128)S(1)}, u32[]{:S(2)}, u32[]{:S(2)}) async-start(s32[64,1,128]{2,1,0:T(1,128)} %broadcast_in_dim.2), calls=%async_computation | async-start | bytes 65536 | tf_op jit(solution)/shard_map/all_to_all | solution.py:342
  36.2 8.0 %collective-permute-start.2 = (f32[23,8,128]{2,1,0:T(8,128)S(1)}, f32[23,8,128]{2,1,0:T(8,128)S(1)}, u32[]{:S(2)}, u32[]{:S(2)}) collective-permute-start(f32[23,8,128]{2,1,0:T(8,128)S(1)} %get-tuple-element.19), channel_id=1, source_target_pairs={{0,2},{1,3},{2,4},{3,5},{4,6},{5,7},{6,8},{7,9},{8,10},{9,11},{10,... | collective-permute-start | bytes 282632 | tf_op jit(solution)/shard_map/ppermute | solution.py:337
  41.7 10.1 %collective-permute-start.3 = (f32[23,8,128]{2,1,0:T(8,128)S(1)}, f32[23,8,128]{2,1,0:T(8,128)S(1)}, u32[]{:S(2)}, u32[]{:S(2)}) collective-permute-start(f32[23,8,128]{2,1,0:T(8,128)S(1)} %get-tuple-element.20), channel_id=1, source_target_pairs={{2,0},{3,1},{4,2},{5,3},{6,4},{7,5},{8,6},{9,7},{10,8},{11,9},{12,... | collective-permute-start | bytes 282632 | tf_op jit(solution)/shard_map/ppermute | solution.py:337
  60.3 0.6 copy-start.1
